TPU v7x, 512 devices: a whole 4x4x16 slice. The times are simulated.
512 devices in a mesh: llm: 16 (over z), enc: 32 (over y, x, core).
Axes of the slice: x: 4, y: 4, z: 16, core: 2. Of those that a mesh axis runs over, the one named last changes fastest.
Arguments:
- frame_counts: int32 [16, 2], P('llm'), may hold values from 1 to 2048, as said below
- dest_rank: int32 [16, 2048, 2, 1], P('llm', 'enc'), may hold values from 0 to 15; in each aligned block of 128 rows (0 to 127, 128 to 255, ..., all dimensions but the last counted through in order) at most 12 rows name the same one
- grad_rows: bfloat16 [16, 16, 384, 2048], P('llm', None, 'enc'), may hold values from -6 to 6
- queries: bfloat16 [16, 2048, 2, 640], P('llm', 'enc'), may hold values from -200 to 200
- key_rows: bfloat16 [16, 2048, 2, 640], P('llm', 'enc'), may hold values from -5 to 5
- value_rows: bfloat16 [16, 2048, 2, 640], P('llm', 'enc'), may hold values from -6 to 6
- conv2_pre: bfloat16 [16, 2048, 2, 640], P('llm', 'enc'), may hold values from -6 to 6
- conv1_pre: bfloat16 [16, 4096, 2, 640], P('llm', 'enc'), may hold values from -6 to 6
- norm_gain: float32 [640], replicated, may hold values from 0.25 to 1.75
- w_proj: bfloat16 [640, 2048], P(None, 'llm'), may hold values from -0.125 to 0.125
- w_out: bfloat16 [640, 640], P('llm'), may hold values from -0.25 to 0.25
- w_qkv: bfloat16 [3, 640, 640], P(None, 'llm'), may hold values from -0.25 to 0.25
- w_conv2: bfloat16 [3, 640, 640], P(None, 'llm'), may hold values from -0.125 to 0.125
- w_conv1: bfloat16 [3, 128, 640], P(None, 'llm'), may hold values from -0.125 to 0.125
Outputs:
- mel_grad: float32 [16, 4096, 2, 128], P('llm', 'enc')
Inputs may be any that keep to these rules, and one draw needn't show every extreme that they name: `dest_rank`: in the 128 frames of one device block of one group, at most 12 name the same LLM rank, a bound that some block reaches. `frame_counts`: in each group one clip, drawn at random, has all 2048 frames.
All inputs are finite; a program needn't handle non-finite values.
Results may differ from a plain program's by a relative error of at most 0.012.
Values may be sent and summed in bfloat16 or wider, within the bound.
A program may use at most 64 MiB of HBM per device.

v0:
```python
import math

import jax
import jax.numpy as jnp
from jax import lax
from jax.sharding import PartitionSpec as P

HEAD_DIM = 40


inv_root_two = 0.7071067811865476
inv_root_two_pi = 0.3989422804014327


def padded(cells, sides, width):
    for axis, dim in sides:
        count = lax.axis_size(axis)
        ends = count - 1
        head = lax.slice_in_dim(cells, 0, width, axis=dim)
        tail = lax.slice_in_dim(cells, cells.shape[dim] - width, cells.shape[dim], axis=dim)
        cells = jnp.concatenate(
            [
                lax.ppermute(tail, axis, [(i, (i + 1) % count) for i in range(ends)]),
                cells,
                lax.ppermute(head, axis, [((i + 1) % count, i) for i in range(ends)]),
            ],
            axis=dim,
        )
    return cells


def gelu_value(value):
    return value * 0.5 * (1.0 + lax.erf(value * inv_root_two))


def gelu_slope(value):
    return (
        0.5 * (1.0 + lax.erf(value * inv_root_two))
        + value * jnp.exp(-0.5 * value * value) * inv_root_two_pi
    )


def positional(places, width):
    halfwidth = width // 2
    ladder = jnp.arange(halfwidth).astype(jnp.float32)
    inverse = jnp.exp(-jnp.log(jnp.float32(10000.0)) * ladder / (halfwidth - 1))
    angle = places.astype(jnp.float32)[:, None] * inverse[None, :]
    return jnp.concatenate([jnp.sin(angle), jnp.cos(angle)], axis=-1)


def attend(pieces):
    query, keyed, valued, d_out, key_valid = pieces
    scale = HEAD_DIM ** (-0.5)
    length = query.shape[0]
    pairs = query.shape[1]
    depth = query.shape[2]
    block = math.gcd(length, 512)
    count = length // block
    keep = jnp.transpose(key_valid[:, :, 0]) > 0
    query_blocks = query.reshape(count, block, pairs, depth)
    d_blocks = d_out.reshape(count, block, pairs, depth)

    def step(carry, parts):
        key_acc, value_acc = carry
        query_part, d_part = parts
        scores = (
            jnp.einsum("qnd,knd->nqk", query_part, keyed, preferred_element_type=jnp.float32)
            * scale
        )
        scores = jnp.where(keep[:, None, :], scores, jnp.float32(-jnp.inf))
        highest = jnp.max(scores, axis=-1, keepdims=True)
        weights = jnp.exp(scores - highest)
        probs = weights / jnp.sum(weights, axis=-1, keepdims=True)
        probs_b = probs.astype(jnp.bfloat16)
        attn_o = jnp.einsum("nqk,knd->qnd", probs_b, valued, preferred_element_type=jnp.float32)
        delta = jnp.sum(d_part.astype(jnp.float32) * attn_o, axis=-1)
        value_acc = value_acc + jnp.einsum(
            "nqk,qnd->knd", probs_b, d_part, preferred_element_type=jnp.float32
        )
        d_probs = jnp.einsum("qnd,knd->nqk", d_part, valued, preferred_element_type=jnp.float32)
        d_scores = (probs * (d_probs - jnp.transpose(delta)[:, :, None]) * scale).astype(
            jnp.bfloat16
        )
        d_query = jnp.einsum(
            "nqk,knd->qnd", d_scores, keyed, preferred_element_type=jnp.float32
        ).astype(jnp.bfloat16)
        key_acc = key_acc + jnp.einsum(
            "nqk,qnd->knd", d_scores, query_part, preferred_element_type=jnp.float32
        )
        return ((key_acc, value_acc), d_query)

    zeros = jnp.zeros((length, pairs, depth), jnp.float32)
    (key_acc, value_acc), d_query = lax.scan(step, (zeros, zeros), (query_blocks, d_blocks))
    return (
        d_query.reshape(length, pairs, depth),
        key_acc.astype(jnp.bfloat16),
        value_acc.astype(jnp.bfloat16),
    )


def per_device(
    frame_counts,
    dest_rank,
    grad_rows,
    queries,
    key_rows,
    value_rows,
    conv2_pre,
    conv1_pre,
    norm_gain,
    w_proj,
    w_out,
    w_qkv,
    w_conv2,
    w_conv1,
):
    groups = lax.axis_size("llm")
    shards = lax.axis_size("enc")
    shard_index = lax.axis_index("enc")
    frames = conv2_pre.shape[1]
    clips = conv2_pre.shape[2]
    width = conv2_pre.shape[3]
    heads = width // HEAD_DIM
    capacity = grad_rows.shape[2]
    row_count = frames * clips
    counts = frame_counts[0]
    places = shard_index * frames + lax.iota(jnp.int32, frames)
    valid = places[:, None] < counts[None, :]
    valid_flat = valid.reshape(-1)
    valid_bf = valid_flat.astype(jnp.bfloat16)[:, None]
    target = dest_rank[0, :, :, 0].reshape(-1)
    onehot = (
        (target[:, None] == lax.iota(jnp.int32, groups)[None, :]) & valid_flat[:, None]
    ).astype(jnp.float32)
    ladder = lax.iota(jnp.int32, row_count)
    lower = (ladder[:, None] >= ladder[None, :]).astype(jnp.float32)
    running = jnp.dot(lower, onehot, precision=lax.Precision.HIGHEST)
    ranks = (jnp.sum(running * onehot, axis=-1) - 1.0).astype(jnp.int32)
    slot = jnp.where(valid_flat, target * capacity + ranks, 0)
    proj_all, out_all, qkv_all, conv_two, conv_one = (
        lax.all_gather(w_proj, "llm", axis=1, tiled=True),
        lax.all_gather(w_out, "llm", axis=0, tiled=True),
        lax.all_gather(w_qkv, "llm", axis=1, tiled=True),
        lax.all_gather(w_conv2, "llm", axis=1, tiled=True),
        lax.all_gather(w_conv1, "llm", axis=1, tiled=True),
    )
    arrived = lax.all_to_all(grad_rows, "llm", split_axis=1, concat_axis=0, tiled=True)
    picked = jnp.take(arrived.reshape(-1, arrived.shape[3]), slot, axis=0) * valid_bf
    upstream = jnp.einsum("fh,dh->fd", picked, proj_all, preferred_element_type=jnp.float32).astype(
        jnp.bfloat16
    )
    d_attn = jnp.einsum("fo,io->fi", upstream, out_all, preferred_element_type=jnp.float32).astype(
        jnp.bfloat16
    )
    pairs = clips * heads
    query = queries[0].reshape(frames, pairs, HEAD_DIM)
    keyed = key_rows[0].reshape(frames, pairs, HEAD_DIM)
    valued = value_rows[0].reshape(frames, pairs, HEAD_DIM)
    d_out = d_attn.reshape(frames, pairs, HEAD_DIM)
    key_valid = jnp.repeat(valid, heads, axis=1)[:, :, None].astype(jnp.bfloat16)
    grads = attend(
        (
            lax.all_to_all(query, "enc", split_axis=1, concat_axis=0, tiled=True),
            lax.all_to_all(keyed, "enc", split_axis=1, concat_axis=0, tiled=True),
            lax.all_to_all(valued, "enc", split_axis=1, concat_axis=0, tiled=True),
            lax.all_to_all(d_out, "enc", split_axis=1, concat_axis=0, tiled=True),
            lax.all_to_all(key_valid, "enc", split_axis=1, concat_axis=0, tiled=True),
        )
    )
    d_query, d_key, d_value = (
        lax.all_to_all(grads[0], "enc", split_axis=0, concat_axis=1, tiled=True),
        lax.all_to_all(grads[1], "enc", split_axis=0, concat_axis=1, tiled=True),
        lax.all_to_all(grads[2], "enc", split_axis=0, concat_axis=1, tiled=True),
    )
    stacked = jnp.stack(
        [
            d_query.reshape(row_count, width),
            d_key.reshape(row_count, width),
            d_value.reshape(row_count, width),
        ],
        axis=1,
    )
    d_normed = jnp.einsum(
        "fjo,jio->fi", stacked, qkv_all, preferred_element_type=jnp.float32
    ).reshape(frames, clips, width)
    pre_two = conv2_pre[0].astype(jnp.float32)
    layer_in = gelu_value(pre_two) + positional(places, width)[:, None, :]
    center = jnp.mean(layer_in, axis=-1, keepdims=True)
    spread = jnp.mean((layer_in - center) ** 2, axis=-1, keepdims=True)
    rstd = 1.0 / jnp.sqrt(spread + 1e-05)
    normed = (layer_in - center) * rstd
    scaled = d_normed * norm_gain
    d_layer = rstd * (
        scaled
        - jnp.mean(scaled, axis=-1, keepdims=True)
        - normed * jnp.mean(scaled * normed, axis=-1, keepdims=True)
    )
    d_conv2 = (
        (upstream.astype(jnp.float32).reshape(frames, clips, width) + d_layer) * gelu_slope(pre_two)
    ).astype(jnp.bfloat16)
    pre_one = conv1_pre[0]
    joined = jnp.concatenate([d_conv2[:, None], pre_one.reshape(frames, 2, clips, width)], axis=1)
    extended = padded(joined, (("enc", 0),), 1)
    conv_rows = extended[:, 0]
    pre_wide = jnp.concatenate([extended[0, 2:3], pre_one, extended[frames + 1, 1:2]], axis=0)
    taps = jnp.einsum("tco,kio->ktci", conv_rows, conv_two, preferred_element_type=jnp.float32)
    odd = taps[2, : frames + 1] + taps[0, 1:]
    even = taps[1, 1:]
    d_hidden = jnp.stack([odd, even], axis=1).reshape(2 * frames + 2, clips, width)
    wide_places = shard_index * 2 * frames - 1 + lax.iota(jnp.int32, 2 * frames + 2)
    inside = ((wide_places >= 0) & (wide_places < 2 * frames * shards)).astype(jnp.bfloat16)[
        :, None, None
    ]
    d_conv1 = (d_hidden * gelu_slope(pre_wide.astype(jnp.float32))).astype(jnp.bfloat16) * inside
    mel_taps = jnp.einsum("sci,kmi->kscm", d_conv1, conv_one, preferred_element_type=jnp.float32)
    mel_grad = mel_taps[0, 2:] + mel_taps[1, 1:-1] + mel_taps[2, :-2]
    return mel_grad[None]


def solution(mesh):
    placed = (
        P("llm", None),
        P("llm", "enc", None, None),
        P("llm", None, "enc", None),
        P("llm", "enc", None, None),
        P("llm", "enc", None, None),
        P("llm", "enc", None, None),
        P("llm", "enc", None, None),
        P("llm", "enc", None, None),
        P(),
        P(None, "llm"),
        P("llm", None),
        P(None, "llm", None),
        P(None, "llm", None),
        P(None, "llm", None),
    )
    return jax.shard_map(
        per_device,
        mesh=mesh,
        in_specs=placed,
        out_specs=P("llm", "enc", None, None),
        check_vma=False,
    )
```

profile of v0, /device:TPU:1, one launch (start us, length us, event | category | flops | bytes accessed | tf_op | source)
XLA Modules:
  0.0 324.5 jit_solution(10666710039521443788)
XLA Ops:
  9.5 10.4 %all-to-all-start.2 = ((bf16[64,32,1]{0,2,1:T(2,128)(2,1)}), bf16[64,32,1]{0,2,1:T(2,128)(2,1)S(1)}, u32[]{:S(2)}, u32[]{:S(2)}) async-start(bf16[64,32,1]{0,2,1:T(2,128)(2,1)} %copy.115), calls=%async_computation.2 | async-start | bytes 32768 | tf_op jit(solution)/shard_map/all_to_all | solution.py:167
  19.9 1.1 copy.112
  21.9 4.9 %all-to-all-done.2 = bf16[64,32,1]{0,2,1:T(2,128)(2,1)S(1)} async-done(((bf16[64,32,1]{0,2,1:T(2,128)(2,1)}), bf16[64,32,1]{0,2,1:T(2,128)(2,1)S(1)}, u32[]{:S(2)}, u32[]{:S(2)}) %all-to-all-start.2) | async-done | bytes 4128 | tf_op jit(solution)/shard_map/all_to_all | solution.py:167
  26.8 4.2 %all-to-all-start.1 = ((bf16[32,2,1280]{2,1,0:T(2,128)(2,1)}), bf16[32,2,1280]{2,1,0:T(2,128)(2,1)S(1)}, u32[]{:S(2)}, u32[]{:S(2)}) async-start(bf16[32,2,1280]{2,1,0:T(2,128)(2,1)} %reshape.468), calls=%async_computation.1 | async-start | bytes 327680 | tf_op jit(solution)/shard_map/all_to_all | solution.py:163
  31.0 1.2 copy.117
  33.1 6.0 %all-to-all-done.1 = bf16[32,2,1280]{2,1,0:T(2,128)(2,1)S(1)} async-done(((bf16[32,2,1280]{2,1,0:T(2,128)(2,1)}), bf16[32,2,1280]{2,1,0:T(2,128)(2,1)S(1)}, u32[]{:S(2)}, u32[]{:S(2)}) %all-to-all-start.1) | async-done | bytes 163872 | tf_op jit(solution)/shard_map/all_to_all | solution.py:163
  39.1 3.8 %all-to-all-start.3 = ((bf16[32,2,1280]{2,1,0:T(2,128)(2,1)}), bf16[32,2,1280]{2,1,0:T(2,128)(2,1)S(1)}, u32[]{:S(2)}, u32[]{:S(2)}) async-start(bf16[32,2,1280]{2,1,0:T(2,128)(2,1)} %reshape.470), calls=%async_computation.3 | async-start | bytes 327680 | tf_op jit(solution)/shard_map/all_to_all | solution.py:164
  42.9 1.1 copy.121
  44.9 5.9 %all-to-all-done.3 = bf16[32,2,1280]{2,1,0:T(2,128)(2,1)S(1)} async-done(((bf16[32,2,1280]{2,1,0:T(2,128)(2,1)}), bf16[32,2,1280]{2,1,0:T(2,128)(2,1)S(1)}, u32[]{:S(2)}, u32[]{:S(2)}) %all-to-all-start.3) | async-done | bytes 163872 | tf_op jit(solution)/shard_map/all_to_all | solution.py:164
  50.9 3.8 %all-to-all-start.5 = ((bf16[32,2,1280]{2,1,0:T(2,128)(2,1)}), bf16[32,2,1280]{2,1,0:T(2,128)(2,1)S(1)}, u32[]{:S(2)}, u32[]{:S(2)}) async-start(bf16[32,2,1280]{2,1,0:T(2,128)(2,1)} %reshape.474), calls=%async_computation.5 | async-start | bytes 327680 | tf_op jit(solution)/shard_map/all_to_all | solution.py:165
  54.7 1.5 copy.109
  56.2 6.4 %all-to-all-done.5 = bf16[32,2,1280]{2,1,0:T(2,128)(2,1)S(1)} async-done(((bf16[32,2,1280]{2,1,0:T(2,128)(2,1)}), bf16[32,2,1280]{2,1,0:T(2,128)(2,1)S(1)}, u32[]{:S(2)}, u32[]{:S(2)}) %all-to-all-start.5) | async-done | bytes 163872 | tf_op jit(solution)/shard_map/all_to_all | solution.py:165
  62.7 13.0 %all-to-all-start = ((bf16[1,16,12,2048]{3,2,0,1:T(8,128)(2,1)}), bf16[1,16,12,2048]{3,2,0,1:T(8,128)(2,1)S(1)}, u32[]{:S(2)}, u32[]{:S(2)}) async-start(bf16[1,16,12,2048]{3,2,0,1:T(8,128)(2,1)} %copy.109), calls=%async_computation | async-start | bytes 2097152 | tf_op jit(solution)/shard_map/all_to_all | solution.py:147
  78.9 74.6 %all_gather.16 = bf16[640,640]{1,0:T(8,128)(2,1)} all-gather(bf16[40,640]{1,0:T(8,128)(2,1)S(1)} %copy-done.10), channel_id=1, replica_groups=mesh['llm'=16,'enc'=32] {'llm'}, dimensions={0}, use_global_device_ids=true | all-gather | bytes 870400 | tf_op jit(solution)/shard_map/all_gather | solution.py:142
  155.9 1.8 gather_fusion
  157.7 2.9 convolution_convert_fusion.2
  163.5 11.6 %all-to-all-start.4 = ((bf16[32,2,1280]{2,1,0:T(2,128)(2,1)}), bf16[32,2,1280]{2,1,0:T(2,128)(2,1)S(1)}, u32[]{:S(2)}, u32[]{:S(2)}) async-start(bf16[32,2,1280]{2,1,0:T(2,128)(2,1)} %reshape.472), calls=%async_computation.4 | async-start | bytes 327680 | tf_op jit(solution)/shard_map/all_to_all | solution.py:166
  175.4 7.5 %all-to-all-done.4 = bf16[32,2,1280]{2,1,0:T(2,128)(2,1)S(1)} async-done(((bf16[32,2,1280]{2,1,0:T(2,128)(2,1)}), bf16[32,2,1280]{2,1,0:T(2,128)(2,1)S(1)}, u32[]{:S(2)}, u32[]{:S(2)}) %all-to-all-start.4) | async-done | bytes 163872 | tf_op jit(solution)/shard_map/all_to_all | solution.py:166
  183.5 38.7 %while.15 = (s32[]{:T(128)}, f32[2048,1,40]{0,2,1:T(8,128)S(1)}, f32[2048,1,40]{0,2,1:T(8,128)S(1)}, bf16[4,512,1,40]{1,3,2,0:T(8,128)(2,1)}, bf16[4,512,1,40]{1...) while((s32[]{:T(128)}, f32[2048,1,40]{0,2,1:T(8,128)S(1)}, ...), condition=%wide.region_7.8_spmd.clone, body=%wide.region_3.7_spmd.clone.sunk | while | flops 521550336 | bytes 71444160 | solution.py:93
  183.6 1.6 fusion.128
  185.2 0.9 fusion.129
  187.9 1.3 copy-done
  189.9 1.4 fusion.132
  191.3 1.4 fusion.134
  193.3 1.6 fusion.128
  194.9 0.9 fusion.129
  197.6 1.3 copy-done
  199.6 1.4 fusion.132
  201.0 1.4 fusion.134
  202.9 1.6 fusion.128
  204.6 0.9 fusion.129
  207.2 1.3 copy-done
  209.3 1.4 fusion.132
  210.7 1.4 fusion.134
  212.6 1.6 fusion.128
  216.9 1.3 copy-done
  218.9 1.4 fusion.132
  220.4 1.4 fusion.134
  223.8 1.4 reshape.478
  225.2 3.8 %all-to-all-start.7 = ((bf16[32,2,1280]{2,1,0:T(2,128)(2,1)}), bf16[32,2,1280]{2,1,0:T(2,128)(2,1)S(1)}, u32[]{:S(2)}, u32[]{:S(2)}) async-start(bf16[32,2,1280]{2,1,0:T(2,128)(2,1)} %reshape.478), calls=%async_computation.7 | async-start | bytes 327680 | tf_op jit(solution)/shard_map/all_to_all | solution.py:172
  229.2 1.2 copy.137
  230.4 1.2 multiply_reduce_fusion.1
  232.6 1.5 reshape.476
  234.1 2.9 all-to-all-done.7
  237.0 4.5 %all-to-all-start.8 = ((bf16[32,2,1280]{2,1,0:T(2,128)(2,1)}), bf16[32,2,1280]{2,1,0:T(2,128)(2,1)S(1)}, u32[]{:S(2)}, u32[]{:S(2)}) async-start(bf16[32,2,1280]{2,1,0:T(2,128)(2,1)} %reshape.476), calls=%async_computation.8 | async-start | bytes 327680 | tf_op jit(solution)/shard_map/all_to_all | solution.py:173
  242.3 1.0 add.204
  244.3 1.4 reshape.480
  245.8 3.7 %all-to-all-done.8 = bf16[32,2,1280]{2,1,0:T(2,128)(2,1)S(1)} async-done(((bf16[32,2,1280]{2,1,0:T(2,128)(2,1)}), bf16[32,2,1280]{2,1,0:T(2,128)(2,1)S(1)}, u32[]{:S(2)}, u32[]{:S(2)}) %all-to-all-start.8) | async-done | bytes 163872 | tf_op jit(solution)/shard_map/all_to_all | solution.py:173
  249.5 3.8 %all-to-all-start.6 = ((bf16[32,2,1280]{2,1,0:T(2,128)(2,1)}), bf16[32,2,1280]{2,1,0:T(2,128)(2,1)S(1)}, u32[]{:S(2)}, u32[]{:S(2)}) async-start(bf16[32,2,1280]{2,1,0:T(2,128)(2,1)} %reshape.480), calls=%async_computation.6 | async-start | bytes 327680 | tf_op jit(solution)/shard_map/all_to_all | solution.py:171
  253.3 27.7 %all_gather.19 = bf16[3,128,640]{2,1,0:T(8,128)(2,1)S(1)} all-gather(bf16[3,8,640]{2,1,0:T(8,128)(2,1)S(1)} %copy-done.11), channel_id=1, replica_groups=mesh['llm'=16,'enc'=32] {'llm'}, dimensions={1}, use_global_device_ids=true | all-gather | bytes 522240 | tf_op jit(solution)/shard_map/all_gather | solution.py:145
  281.2 1.5 reshape.479
  283.6 0.9 copy.131
  284.6 1.2 stack_reshape.10
  285.7 1.5 reshape.477
  288.2 0.9 copy.134
  289.1 1.2 stack_reshape.11
  290.3 1.5 reshape.481
  292.8 0.9 copy.128
  294.3 2.8 multiply_reduce_fusion.2
  298.1 7.9 %collective-permute-start = (bf16[1,3,2,640]{3,0,2,1:T(2,128)(2,1)S(1)}, bf16[1,3,2,640]{3,0,2,1:T(2,128)(2,1)S(1)}, u32[]{:S(2)}, u32[]{:S(2)}) collective-permute-start(bf16[1,3,2,640]{3,0,2,1:T(2,128)(2,1)S(1)} %get-tuple-element.138), channel_id=1, source_target_pairs={{0,1},{1,2},{2,3},{3,4},{4,5},{5,6},{6,7},{7,8},{8,9},{9,10},{10,1... | collective-permute-start | bytes 23048 | tf_op jit(solution)/shard_map/ppermute | solution.py:23
  306.0 1.9 collective-permute-start.1
  308.0 3.1 collective-permute-done.1
  311.0 2.8 fusion.30
  314.4 2.4 multiply_bitcast_fusion
  (168 shorter events, 38.1 us)
Async XLA Ops:
  6.5 48.2 %copy-start.4 = (bf16[1,16,12,2048]{3,1,2,0:T(8,128)(2,1)S(1)}, bf16[1,16,12,2048]{3,1,2,0:T(8,128)(2,1)}, u32[]{:S(2)}) copy-start(bf16[1,16,12,2048]{3,1,2,0:T(8,128)(2,1)} %param.18) | copy-start | bytes 2359300
  6.5 151.1 %all-gather.4.cloned.1.call-start = ((), (), s32[]{:S(2)}) async-start(), calls=%async_computation.9 | async-start | bytes 2785280 | tf_op jit(solution)/shard_map/all_gather | solution.py:141
  7.3 69.5 %copy-start.13 = (s32[1,64,2,1]{1,3,2,0:T(1,128)S(1)}, s32[1,64,2,1]{1,3,2,0:T(1,128)}, u32[]{:S(2)}) copy-start(s32[1,64,2,1]{1,3,2,0:T(1,128)} %param.17) | copy-start | bytes 1540
  7.3 287.0 %all-gather.6.cloned.1.call-start = ((), (), s32[]{:S(2)}) async-start(), calls=%async_computation.10 | async-start | bytes 2611200 | tf_op jit(solution)/shard_map/all_gather | solution.py:143
  9.5 17.3 %all-to-all-start.2 = ((bf16[64,32,1]{0,2,1:T(2,128)(2,1)}), bf16[64,32,1]{0,2,1:T(2,128)(2,1)S(1)}, u32[]{:S(2)}, u32[]{:S(2)}) async-start(bf16[64,32,1]{0,2,1:T(2,128)(2,1)} %copy.115), calls=%async_computation.2 | async-start | bytes 32768 | tf_op jit(solution)/shard_map/all_to_all | solution.py:167
  21.0 57.0 %copy-start.5 = (bf16[1,64,2,640]{3,2,1,0:T(2,128)(2,1)S(1)}, bf16[1,64,2,640]{3,2,1,0:T(2,128)(2,1)}, u32[]{:S(2)}) copy-start(bf16[1,64,2,640]{3,2,1,0:T(2,128)(2,1)} %param.22) | copy-start | bytes 491524
  21.9 56.9 %copy-start.10 = (bf16[40,640]{1,0:T(8,128)(2,1)S(1)}, bf16[40,640]{1,0:T(8,128)(2,1)}, u32[]{:S(2)}) copy-start(bf16[40,640]{1,0:T(8,128)(2,1)} %param.26) | copy-start | bytes 153604
  26.8 12.2 %all-to-all-start.1 = ((bf16[32,2,1280]{2,1,0:T(2,128)(2,1)}), bf16[32,2,1280]{2,1,0:T(2,128)(2,1)S(1)}, u32[]{:S(2)}, u32[]{:S(2)}) async-start(bf16[32,2,1280]{2,1,0:T(2,128)(2,1)} %reshape.468), calls=%async_computation.1 | async-start | bytes 327680 | tf_op jit(solution)/shard_map/all_to_all | solution.py:163
  39.1 11.8 %all-to-all-start.3 = ((bf16[32,2,1280]{2,1,0:T(2,128)(2,1)}), bf16[32,2,1280]{2,1,0:T(2,128)(2,1)S(1)}, u32[]{:S(2)}, u32[]{:S(2)}) async-start(bf16[32,2,1280]{2,1,0:T(2,128)(2,1)} %reshape.470), calls=%async_computation.3 | async-start | bytes 327680 | tf_op jit(solution)/shard_map/all_to_all | solution.py:164
  50.9 11.8 %all-to-all-start.5 = ((bf16[32,2,1280]{2,1,0:T(2,128)(2,1)}), bf16[32,2,1280]{2,1,0:T(2,128)(2,1)S(1)}, u32[]{:S(2)}, u32[]{:S(2)}) async-start(bf16[32,2,1280]{2,1,0:T(2,128)(2,1)} %reshape.474), calls=%async_computation.5 | async-start | bytes 327680 | tf_op jit(solution)/shard_map/all_to_all | solution.py:165
  62.7 93.0 %all-to-all-start = ((bf16[1,16,12,2048]{3,2,0,1:T(8,128)(2,1)}), bf16[1,16,12,2048]{3,2,0,1:T(8,128)(2,1)S(1)}, u32[]{:S(2)}, u32[]{:S(2)}) async-start(bf16[1,16,12,2048]{3,2,0,1:T(8,128)(2,1)} %copy.109), calls=%async_computation | async-start | bytes 2097152 | tf_op jit(solution)/shard_map/all_to_all | solution.py:147
  75.7 232.2 %all-gather.8.cloned.1.call-start = ((), (), s32[]{:S(2)}) async-start(), calls=%async_computation.11 | async-start | bytes 2611200 | tf_op jit(solution)/shard_map/all_gather | solution.py:144
  155.9 4.7 %copy-start.2 = (bf16[640,640]{1,0:T(8,128)(2,1)S(1)}, bf16[640,640]{1,0:T(8,128)(2,1)}, u32[]{:S(2)}) copy-start(bf16[640,640]{1,0:T(8,128)(2,1)} %all_gather.16) | copy-start | bytes 2457604
  160.6 0.7 copy-start.7
  163.5 19.5 %all-to-all-start.4 = ((bf16[32,2,1280]{2,1,0:T(2,128)(2,1)}), bf16[32,2,1280]{2,1,0:T(2,128)(2,1)S(1)}, u32[]{:S(2)}, u32[]{:S(2)}) async-start(bf16[32,2,1280]{2,1,0:T(2,128)(2,1)} %reshape.472), calls=%async_computation.4 | async-start | bytes 327680 | tf_op jit(solution)/shard_map/all_to_all | solution.py:166
  187.1 2.0 copy-start
  189.9 2.8 copy-start.1
  196.8 2.0 copy-start
  199.6 2.8 copy-start.1
  206.5 2.0 copy-start
  209.2 2.8 copy-start.1
  216.1 2.0 copy-start
  218.9 2.8 copy-start.1
  222.2 21.0 %copy-start.3 = (bf16[1,128,2,640]{3,2,1,0:T(2,128)(2,1)S(1)}, bf16[1,128,2,640]{3,2,1,0:T(2,128)(2,1)}, u32[]{:S(2)}) copy-start(bf16[1,128,2,640]{3,2,1,0:T(2,128)(2,1)} %param.23) | copy-start | bytes 983044
  222.3 21.0 %copy-start.9 = (bf16[4,512,1,40]{1,3,2,0:T(8,128)(2,1)S(1)}, bf16[4,512,1,40]{1,3,2,0:T(8,128)(2,1)}, u32[]{:S(2)}) copy-start(bf16[4,512,1,40]{1,3,2,0:T(8,128)(2,1)} %get-tuple-element.54) | copy-start | bytes 491524
  225.2 11.8 %all-to-all-start.7 = ((bf16[32,2,1280]{2,1,0:T(2,128)(2,1)}), bf16[32,2,1280]{2,1,0:T(2,128)(2,1)S(1)}, u32[]{:S(2)}, u32[]{:S(2)}) async-start(bf16[32,2,1280]{2,1,0:T(2,128)(2,1)} %reshape.478), calls=%async_computation.7 | async-start | bytes 327680 | tf_op jit(solution)/shard_map/all_to_all | solution.py:172
  229.2 24.1 %copy-start.11 = (bf16[3,8,640]{2,1,0:T(8,128)(2,1)S(1)}, bf16[3,8,640]{2,1,0:T(8,128)(2,1)}, u32[]{:S(2)}) copy-start(bf16[3,8,640]{2,1,0:T(8,128)(2,1)} %param.29) | copy-start | bytes 92164
  230.4 50.6 %copy-start.8 = (bf16[128,640]{1,0:T(8,128)(2,1)S(1)}, bf16[128,640]{1,0:T(8,128)(2,1)}, u32[]{:S(2)}) copy-start(bf16[128,640]{1,0:T(8,128)(2,1)} %copy-done.7) | copy-start | bytes 491524
  237.0 12.4 %all-to-all-start.8 = ((bf16[32,2,1280]{2,1,0:T(2,128)(2,1)}), bf16[32,2,1280]{2,1,0:T(2,128)(2,1)S(1)}, u32[]{:S(2)}, u32[]{:S(2)}) async-start(bf16[32,2,1280]{2,1,0:T(2,128)(2,1)} %reshape.476), calls=%async_computation.8 | async-start | bytes 327680 | tf_op jit(solution)/shard_map/all_to_all | solution.py:173
  249.5 40.9 %all-to-all-start.6 = ((bf16[32,2,1280]{2,1,0:T(2,128)(2,1)}), bf16[32,2,1280]{2,1,0:T(2,128)(2,1)S(1)}, u32[]{:S(2)}, u32[]{:S(2)}) async-start(bf16[32,2,1280]{2,1,0:T(2,128)(2,1)} %reshape.480), calls=%async_computation.6 | async-start | bytes 327680 | tf_op jit(solution)/shard_map/all_to_all | solution.py:171
  285.7 8.5 %copy-start.12 = (f32[640]{0:T(1024)S(1)}, f32[640]{0:T(1024)}, u32[]{:S(2)}) copy-start(f32[640]{0:T(1024)} %param.24) | copy-start | bytes 7684
  291.9 5.8 %copy-start.6 = (bf16[1,64,2,640]{3,2,1,0:T(2,128)(2,1)S(1)}, bf16[1,64,2,640]{3,2,1,0:T(2,128)(2,1)}, u32[]{:S(2)}) copy-start(bf16[1,64,2,640]{3,2,1,0:T(2,128)(2,1)} %param.22) | copy-start | bytes 491524
  298.1 9.9 %collective-permute-start = (bf16[1,3,2,640]{3,0,2,1:T(2,128)(2,1)S(1)}, bf16[1,3,2,640]{3,0,2,1:T(2,128)(2,1)S(1)}, u32[]{:S(2)}, u32[]{:S(2)}) collective-permute-start(bf16[1,3,2,640]{3,0,2,1:T(2,128)(2,1)S(1)} %get-tuple-element.138), channel_id=1, source_target_pairs={{0,1},{1,2},{2,3},{3,4},{4,5},{5,6},{6,7},{7,8},{8,9},{9,10},{10,1... | collective-permute-start | bytes 23048 | tf_op jit(solution)/shard_map/ppermute | solution.py:23
  306.0 5.0 %collective-permute-start.1 = (bf16[1,3,2,640]{3,0,2,1:T(2,128)(2,1)S(1)}, bf16[1,3,2,640]{3,0,2,1:T(2,128)(2,1)S(1)}, u32[]{:S(2)}, u32[]{:S(2)}) collective-permute-start(bf16[1,3,2,640]{3,0,2,1:T(2,128)(2,1)S(1)} %get-tuple-element.139), channel_id=1, source_target_pairs={{1,0},{2,1},{3,2},{4,3},{5,4},{6,5},{7,6},{8,7},{9,8},{10,9},{11,1... | collective-permute-start | bytes 23048 | tf_op jit(solution)/shard_map/ppermute | solution.py:25
Sparse Core Ops, SparseCore 0:
  9.4 112.5 all-gather.3
  124.0 76.6 all-gather.5
  202.8 72.2 all-gather.7
where the time goes:
time: 327 us; the launch traced here: 325 us
  blocking collectives  102 us (31%)
  starting transfers between devices  68.8 us (21%)
  local copies, waits for them, and re-layouts  45.4 us (14%)
  waiting for transfers between devices  42.7 us (13%)
  matrix products  35.1 us (11%)
  other arithmetic  16 us (5%)
  between operations  14 us (4%)
    all_gather x1, blocking collectives, per_device(): lax.all_gather(w_out, 'llm', axis=0, tiled=True)  74.6 us
    all_gather x1, blocking collectives, per_device(): lax.all_gather(w_conv1, 'llm', axis=1, tiled=True)  27.7 us
    unnamed x50, local copies, waits for them, and re-layouts  20.4 us
    all_to_all x1, starting transfers between devices, per_device(): lax.all_to_all(grad_rows, 'llm', split_axis=1, concat_axis=0, tiled=True)  13 us
    all_to_all x1, starting transfers between devices, per_device(): lax.all_to_all(d_out, 'enc', split_axis=1, concat_axis=0, tiled=True)  11.6 us
    all_to_all x1, starting transfers between devices, per_device(): lax.all_to_all(key_valid, 'enc', split_axis=1, concat_axis=0, tiled=True)  10.4 us
    ppermute x1, starting transfers between devices, padded(): lax.ppermute(tail, axis, [(i, (i + 1) % count) for i in range(ends)])  7.92 us
    all_to_all x1, waiting for transfers between devices, per_device(): lax.all_to_all(d_out, 'enc', split_axis=1, concat_axis=0, tiled=True)  7.53 us
  transfers between devices with their start and end apart: 14, of which 8 were waited for; matrix products, arithmetic and copies ran while one was open for 25% of the time, Pallas kernels for 0%

commit v1 on v0

v1 whole, which is shorter than its diff:
```python
import functools

import jax
import jax.numpy as jnp
import numpy as np
from jax import lax
from jax.experimental import pallas as pl
from jax.experimental.pallas import tpu as pltpu
from jax.sharding import PartitionSpec as P

MESH = pl.DeviceIdType.MESH
F32, BF16 = jnp.float32, jnp.bfloat16
HEAD_DIM = 40
WIDTH = 640
HID = 2048
LENGTH = 2048
SCALE = HEAD_DIM ** (-0.5)
LOG2E = 1.4426950408889634
MASKED = -1e30
ROOT_HALF = 0.7071067811865476
INV_ROOT_TWO_PI = 0.3989422804014327
QB = 256


def gelu_value(value):
    return value * 0.5 * (1.0 + lax.erf(value * ROOT_HALF))


def gelu_slope(value):
    return (
        0.5 * (1.0 + lax.erf(value * ROOT_HALF))
        + value * jnp.exp(-0.5 * value * value) * INV_ROOT_TWO_PI
    )


def dot(a, b, dims):
    return lax.dot_general(a, b, (dims, ((), ())), preferred_element_type=F32)


NN = ((1,), (0,))
NT = ((1,), (1,))
TN = ((0,), (0,))


def tables():
    inverse = 10000.0 ** (-np.arange(320) / 319.0)
    base = 128.0 * np.arange(16)[:, None] * inverse[None, :]
    local = np.arange(128.0)[:, None] * inverse[None, :]
    first = np.concatenate([np.sin(base), np.cos(base)], axis=1)
    second = np.concatenate([np.cos(base), -np.sin(base)], axis=1)
    chip = np.stack([first, second], axis=1).astype(np.float32)
    near = np.stack(
        [np.concatenate([np.cos(local)] * 2, 1), np.concatenate([np.sin(local)] * 2, 1)]
    ).astype(np.float32)
    return chip, near


def kernel(
    counts, target, grads, q_in, k_in, v_in, c2_in, c1_in, gain, wp_in, wo_in, wqkv_in, wc2_in, wc1_in,
    chip_tab, near_tab,
    out,
    g_loc, q_loc, k_loc, v_loc, c2_loc, c1_loc, wo_loc, wqkv_loc, wc2_loc, wc1_loc, near,
    w_slab, wp, wr, w_full, w_last,
    cl1, cl2, xb1, xb2, head_send, qkv, kn, vn, qn,
    u_send, u_recv, up_send, up, d_send, d_out, dn,
    e_mat, big, rl, dk_acc, dv_acc, grad_t, grad_recv,
    slope1, halo1, d2_buf, halo2, mel_buf, mel_recv,
    loc_sem, wpz_s, wpz_r, wp1_s, wp1_r, wp2_s, wp2_r, wpc_s, wpc_r,
    wrz_s, wrz_r, wr1_s, wr1_r, wr2_s, wr2_r, wrc_s, wrc_r,
    xs, xr, qs, qr, us, ur, ds_, dr, bs, br, hs, hr,
):
    z = lax.axis_index("llm")
    e = lax.axis_index("enc")
    core = lax.rem(e, 2)
    other = 1 - core
    chip = e // 2
    x = lax.rem(chip, 4)
    y = chip // 4
    a = jnp.where(core == 0, x, y)
    b = jnp.where(core == 0, y, x)
    sibling = (z, chip * 2 + other)

    def along_a(step):
        to = lax.rem(a + step, 4)
        return (z, jnp.where(core == 0, y * 4 + to, to * 4 + x) * 2 + core)

    def along_b(step):
        to = lax.rem(b + step, 4)
        return (z, jnp.where(core == 0, to * 4 + x, y * 4 + to) * 2 + core)

    def on_chip(number):
        return (z, number * 2 + core)

    def remote(src, dst, send, recv, device):
        return pltpu.make_async_remote_copy(
            src_ref=src, dst_ref=dst, send_sem=send, recv_sem=recv, device_id=device, device_id_type=MESH
        )

    loads = [
        (q_in.at[0], q_loc), (k_in.at[0], k_loc), (v_in.at[0], v_loc), (wo_in, wo_loc), (wqkv_in, wqkv_loc),
        (wc2_in, wc2_loc), (wc1_in, wc1_loc), (c2_in.at[0], c2_loc), (c1_in.at[0], c1_loc),
        (grads, g_loc), (near_tab, near),
    ]
    for i, (src, dst) in enumerate(loads):
        pltpu.make_async_copy(src, dst, loc_sem.at[i]).start()

    def loaded(i):
        pltpu.make_async_copy(loads[i][0], loads[i][1], loc_sem.at[i]).wait()

    barrier = pltpu.get_barrier_semaphore()

    def greet(step, carry):
        pl.semaphore_signal(barrier, inc=1, device_id=(lax.rem(z + step, 16), e), device_id_type=MESH)
        pl.semaphore_signal(
            barrier, inc=1, device_id=on_chip(lax.rem(chip + step, 16)), device_id_type=MESH
        )
        return carry

    lax.fori_loop(1, 16, greet, 0)
    pl.semaphore_signal(barrier, inc=1, device_id=sibling, device_id_type=MESH)
    pl.semaphore_wait(barrier, 31)

    piece = 2 * b + a // 2
    kind = lax.rem(a, 2) + 2 * core
    wp_rows = pl.ds(pl.multiple_of(piece * 80, 16), 80)

    def wpz(step, index):
        return remote(
            wp_in.at[wp_rows, :],
            wp.at[wp_rows, pl.ds(pl.multiple_of((kind * 4 + index) * 128, 128), 128)],
            wpz_s.at[step], wpz_r.at[index], (lax.rem(z + step, 16), e),
        )

    wp_sends = lax.rem(z, 4) == kind
    wp_own = pltpu.make_async_copy(
        wp_in.at[wp_rows, :],
        wp.at[wp_rows, pl.ds(pl.multiple_of((kind * 4 + z // 4) * 128, 128), 128)],
        loc_sem.at[11],
    )

    @pl.when(wp_sends)
    def _():
        def body(step, carry):
            wpz(step, z // 4).start()
            return carry

        lax.fori_loop(1, 16, body, 0)
        wp_own.start()

    for i, ref in enumerate((q_loc, k_loc, v_loc)):
        loaded(i)
        for clip in range(2):
            cl1[clip, i * 64 : (i + 1) * 64, :] = ref[:, clip, :]
    swap1 = remote(cl1.at[other], xb1.at[core], xs.at[0], xr.at[0], sibling)
    swap1.start()
    keep1 = pltpu.make_async_copy(cl1.at[core], xb1.at[core], loc_sem.at[12])
    keep1.start()

    for i in range(3, 7):
        loaded(i)
    parts = [wo_loc[...].astype(F32)]
    parts += [wqkv_loc[i].astype(F32) for i in range(3)]
    parts += [wc2_loc[i].astype(F32) for i in range(3)]
    parts += [wc1_loc[i].astype(F32) for i in range(3)]
    parts += [jnp.zeros((16, WIDTH), F32)]
    w_slab[...] = jnp.concatenate(parts, axis=0).astype(BF16)
    group8 = a + 4 * core
    wr_rows = pl.ds(pl.multiple_of(b * 80, 16), 80)

    def wrz(step, index):
        return remote(
            w_slab.at[wr_rows, :], wr.at[group8 * 2 + index, wr_rows, :],
            wrz_s.at[step], wrz_r.at[index], (lax.rem(z + step, 16), e),
        )

    wr_sends = lax.rem(z, 8) == group8
    wr_own = pltpu.make_async_copy(
        w_slab.at[wr_rows, :], wr.at[group8 * 2 + z // 8, wr_rows, :], loc_sem.at[13]
    )

    @pl.when(wr_sends)
    def _():
        def body(step, carry):
            wrz(step, z // 8).start()
            return carry

        lax.fori_loop(1, 16, body, 0)
        wr_own.start()

    for index in range(4):
        @pl.when(kind + 4 * index != z)
        def _():
            wpz(1, index).wait_recv()

    @pl.when(wp_sends)
    def _():
        wp_own.wait()

    def wp1(step):
        block = wp.at[wp_rows, pl.ds(pl.multiple_of(kind * 512, 128), 512)]
        return remote(block, block, wp1_s.at[step], wp1_r.at[step], along_a(step))

    for step in range(1, 4):
        wp1(step).start()

    swap1.wait_recv()
    keep1.wait()
    places = chip * 128 + lax.broadcasted_iota(jnp.int32, (8, 128), 1)
    row8 = lax.broadcasted_iota(jnp.int32, (8, 128), 0)
    own_count = jnp.where(core == 0, counts[0, 0], counts[0, 1])
    ones_rows = jnp.where(row8 == 0, 1.0, 0.0)
    bias_rows = jnp.where((row8 == 0) & (places >= own_count), MASKED, 0.0)
    zero_rows = jnp.zeros((8, 128), F32)
    for i, extra in enumerate((ones_rows, bias_rows, zero_rows)):
        rows = jnp.concatenate(
            [xb1[0, i * 64 : (i + 1) * 64, :], xb1[1, i * 64 : (i + 1) * 64, :]], axis=0
        ).astype(F32)
        turned = jnp.transpose(rows)
        for head in range(16):
            head_send[head, i * 48 : (i + 1) * 48, :] = jnp.concatenate(
                [turned[head * 40 : head * 40 + 40], extra], axis=0
            ).astype(BF16)
    chip_lanes = pl.ds(pl.multiple_of(chip * 128, 128), 128)

    def qkv_copy(step):
        to = lax.rem(chip + step, 16)
        return remote(head_send.at[to], qkv.at[:, chip_lanes], qs.at[step], qr.at[step], on_chip(to))

    def start_qkv(step, carry):
        qkv_copy(step).start()
        return carry

    lax.fori_loop(1, 16, start_qkv, 0)
    qkv_own = pltpu.make_async_copy(head_send.at[chip], qkv.at[:, chip_lanes], loc_sem.at[14])
    qkv_own.start()

    for step in range(1, 4):
        wp1(step).wait_recv()

    def wp_set(number):
        return wp.at[
            pl.ds(pl.multiple_of(number * 160, 16), 160), pl.ds(pl.multiple_of(core * 1024, 128), 1024)
        ]

    def wp2(step):
        return remote(wp_set(b), wp_set(b), wp2_s.at[step], wp2_r.at[step], along_b(step))

    def wpc(step):
        held = wp_set(lax.rem(b - step + 4, 4))
        return remote(held, held, wpc_s.at[step], wpc_r.at[step], sibling)

    for step in range(1, 4):
        wp2(step).start()
    wpc(0).start()

    loaded(7)
    loaded(8)
    for clip in range(2):
        cl2[clip, 0:64, :] = c2_loc[:, clip, :]
        cl2[clip, 64:192, :] = c1_loc[:, clip, :]
    swap2 = remote(cl2.at[other], xb2.at[core], xs.at[1], xr.at[1], sibling)
    swap2.start()
    keep2 = pltpu.make_async_copy(cl2.at[core], xb2.at[core], loc_sem.at[15])
    keep2.start()

    for index in range(2):
        @pl.when(group8 + 8 * index != z)
        def _():
            wrz(1, index).wait_recv()

    @pl.when(wr_sends)
    def _():
        wr_own.wait()

    def wr1(step):
        block = wr.at[pl.ds(group8 * 2, 2), wr_rows, :]
        return remote(block, block, wr1_s.at[step], wr1_r.at[step], along_a(step))

    for step in range(1, 4):
        wr1(step).start()

    for step in range(1, 4):
        wp2(step).wait_recv()
        wpc(step).start()

    loaded(9)
    for step in range(4):
        wpc(step).wait_recv()

    total = jnp.zeros((192, WIDTH), F32)
    for number in range(4):
        rows = jnp.concatenate(
            [g_loc[:, (number + 4 * i) * 128 : (number + 4 * i + 1) * 128] for i in range(4)], axis=1
        )
        total = total + dot(rows, wp[:, number * 512 : (number + 1) * 512], NT)
    slot_row = lax.broadcasted_iota(jnp.int32, (256, 192), 0)
    held_row = lax.broadcasted_iota(jnp.int32, (256, 192), 1)
    order = (lax.rem(slot_row, 16) * 16 + slot_row // 16 == held_row).astype(F32).astype(BF16)
    u_send[...] = dot(order, total.astype(BF16), NN).astype(BF16).reshape(16, 16, WIDTH)

    def u_copy(step):
        to = lax.rem(z + step, 16)
        return remote(u_send.at[to], u_recv.at[z], us.at[step], ur.at[step], (to, e))

    def start_u(step, carry):
        u_copy(step).start()
        return carry

    lax.fori_loop(1, 16, start_u, 0)
    u_own = pltpu.make_async_copy(u_send.at[z], u_recv.at[z], loc_sem.at[16])
    u_own.start()

    for step in range(1, 4):
        wr1(step).wait_recv()

    def wr_set(number):
        return wr.at[pl.ds(core * 8, 8), pl.ds(pl.multiple_of(number * 80, 16), 80), :]

    def wr2(step):
        return remote(wr_set(b), wr_set(b), wr2_s.at[step], wr2_r.at[step], along_b(step))

    def wrc(step):
        held = wr_set(lax.rem(b - step + 4, 4))
        return remote(held, held, wrc_s.at[step], wrc_r.at[step], sibling)

    for step in range(1, 4):
        wr2(step).start()
    wrc(0).start()

    swap2.wait_recv()
    keep2.wait()
    after = on_chip(lax.rem(chip + 1, 16))
    before = on_chip(lax.rem(chip + 15, 16))
    edge_up = remote(xb2.at[1, pl.ds(176, 16), :], halo1.at[0], hs.at[0], hr.at[0], after)
    edge_down = remote(xb2.at[0, pl.ds(64, 16), :], halo1.at[1], hs.at[1], hr.at[1], before)
    edge_up.start()
    edge_down.start()

    def wait_qkv(step, carry):
        qkv_copy(step).wait_recv()
        return carry

    lax.fori_loop(1, 16, wait_qkv, 0)
    qkv_own.wait()
    qn[...] = jnp.transpose(qkv[0:48, :].astype(F32)).astype(BF16)
    kn[...] = jnp.transpose(qkv[48:96, :].astype(F32)).astype(BF16)
    vn[...] = jnp.transpose(qkv[96:144, :].astype(F32)).astype(BF16)

    def exponentials(number, carry):
        lanes = pl.ds(pl.multiple_of(number * QB, QB), QB)
        big[...] = dot(kn[...], qkv[0:48, lanes], NN)
        highest = jnp.max(big[...], axis=0, keepdims=True)
        weights = jnp.exp2((big[...] - highest) * (SCALE * LOG2E))
        e_mat[:, lanes] = weights.astype(BF16)
        rl[:, lanes] = 1.0 / jnp.sum(weights, axis=0, keepdims=True)
        return carry

    lax.fori_loop(0, LENGTH // QB, exponentials, 0)

    for step in range(1, 4):
        wr2(step).wait_recv()
        wrc(step).start()
    for step in range(4):
        wrc(step).wait_recv()

    def compact(number, carry):
        first = 2 * number
        slabs = []
        for place in (first, first + 1):
            slabs.append(wr[lax.rem(place, 8) * 2 + place // 8].astype(F32))
        rows = pl.ds(pl.multiple_of(number * 80, 16), 80)
        for i in range(7):
            w_full[i, rows, :] = jnp.concatenate(
                [slab[i * 40 : i * 40 + 40] for slab in slabs], axis=0
            ).astype(BF16)
        for i in range(3):
            w_last[pl.ds(pl.multiple_of(i * 128 + number * 16, 16), 16), :] = jnp.concatenate(
                [slab[280 + i * 8 : 288 + i * 8] for slab in slabs], axis=0
            ).astype(BF16)
        return carry

    lax.fori_loop(0, 8, compact, 0)

    slots = lax.broadcasted_iota(jnp.int32, (256, 64), 0)
    frame = e * 64 + lax.broadcasted_iota(jnp.int32, (256, 64), 1)
    named = []
    for clip in range(2):
        hit = (target[clip : clip + 1, :] == slots // 16) & (frame < counts[0, clip])
        named.append(jnp.where(hit, 1.0, 0.0))
    earlier = lax.broadcasted_iota(jnp.int32, (64, 64), 0)
    later = lax.broadcasted_iota(jnp.int32, (64, 64), 1)
    upto = (earlier <= later).astype(F32).astype(BF16)
    under = (earlier < later).astype(F32).astype(BF16)
    named_b = [part.astype(BF16) for part in named]
    seen = [
        dot(named_b[0], upto, NN) + dot(named_b[1], under, NN),
        dot(named_b[0], upto, NN) + dot(named_b[1], upto, NN),
    ]
    within = lax.rem(slots, 16).astype(F32) + 1.0
    choose = jnp.concatenate(
        [jnp.where(seen[i] == within, named[i], 0.0) for i in range(2)], axis=1
    ).astype(BF16)

    def wait_u(step, carry):
        u_copy(step).wait_recv()
        return carry

    lax.fori_loop(1, 16, wait_u, 0)
    u_own.wait()
    up_send[...] = (
        dot(choose, u_recv[...].reshape(256, WIDTH), TN).astype(BF16).reshape(2, 64, WIDTH)
    )
    swap3 = remote(up_send.at[other], up.at[core], xs.at[2], xr.at[2], sibling)
    swap3.start()
    keep3 = pltpu.make_async_copy(up_send.at[core], up.at[core], loc_sem.at[17])
    keep3.start()
    swap3.wait_recv()
    keep3.wait()
    d_attn = dot(w_full[0], up[...].reshape(128, WIDTH), NT)
    for head in range(16):
        d_send[head] = jnp.concatenate([d_attn[head * 40 : head * 40 + 40], zero_rows], axis=0).astype(
            BF16
        )

    def d_copy(step):
        to = lax.rem(chip + step, 16)
        return remote(d_send.at[to], d_out.at[:, chip_lanes], ds_.at[step], dr.at[step], on_chip(to))

    def start_d(step, carry):
        d_copy(step).start()
        return carry

    lax.fori_loop(1, 16, start_d, 0)
    d_own = pltpu.make_async_copy(d_send.at[chip], d_out.at[:, chip_lanes], loc_sem.at[18])
    d_own.start()

    edge_up.wait_recv()
    edge_down.wait_recv()
    for i in range(5):
        lanes = slice(i * 128, i * 128 + 128)
        slope1[i, 0:16, :] = gelu_slope(halo1[0, :, lanes].astype(F32))
        slope1[i, 16:144, :] = gelu_slope(xb2[0, 64:192, lanes].astype(F32))
        slope1[i, 144:272, :] = gelu_slope(xb2[1, 64:192, lanes].astype(F32))
        slope1[i, 272:288, :] = gelu_slope(halo1[1, :, lanes].astype(F32))

    def wait_d(step, carry):
        d_copy(step).wait_recv()
        return carry

    lax.fori_loop(1, 16, wait_d, 0)
    d_own.wait()
    shared = d_out[...].astype(F32) * rl[...]
    d_out[...] = shared.astype(BF16)
    dn[...] = jnp.transpose(shared).astype(BF16)
    dk_acc[...] = jnp.zeros_like(dk_acc)
    dv_acc[...] = jnp.zeros_like(dv_acc)

    def gradients(number, carry):
        lanes = pl.ds(pl.multiple_of(number * QB, QB), QB)
        weights = e_mat[:, lanes]
        big[...] = dot(vn[...], d_out[:, lanes], NN)
        delta = jnp.sum(weights.astype(F32) * big[...], axis=0, keepdims=True) * rl[:, lanes]
        slopes = (weights.astype(F32) * (big[...] - delta)).astype(BF16)
        dv_acc[...] += dot(weights, dn[lanes, :], NN)
        dk_acc[...] += dot(slopes, qn[lanes, :], NN)
        grad_t[0:48, lanes] = (dot(qkv[48:96, :], slopes, NN) * SCALE).astype(BF16)
        return carry

    lax.fori_loop(0, LENGTH // QB, gradients, 0)
    grad_t[48:96, :] = jnp.transpose(dk_acc[...] * SCALE).astype(BF16)
    grad_t[96:144, :] = jnp.transpose(dv_acc[...]).astype(BF16)

    def grad_lanes(number):
        return grad_t.at[:, pl.ds(pl.multiple_of(number * 128, 128), 128)]

    def b_copy(step):
        to = lax.rem(chip + step, 16)
        return remote(grad_lanes(to), grad_recv.at[chip], bs.at[step], br.at[step], on_chip(to))

    def start_b(step, carry):
        b_copy(step).start()
        return carry

    lax.fori_loop(1, 16, start_b, 0)
    b_own = pltpu.make_async_copy(grad_lanes(chip), grad_recv.at[chip], loc_sem.at[19])
    b_own.start()

    loaded(10)
    pre_two = jnp.concatenate([xb2[0, 0:64, :], xb2[1, 0:64, :]], axis=0).astype(F32)
    pair = chip_tab[chip]
    layer_in = gelu_value(pre_two) + pair[0:1] * near[0] + pair[1:2] * near[1]
    center = jnp.mean(layer_in, axis=-1, keepdims=True)
    moved = layer_in - center
    rstd = 1.0 / jnp.sqrt(jnp.mean(moved * moved, axis=-1, keepdims=True) + 1e-05)
    normed = moved * rstd

    def wait_b(step, carry):
        b_copy(step).wait_recv()
        return carry

    lax.fori_loop(1, 16, wait_b, 0)
    b_own.wait()
    d_normed = jnp.zeros((128, WIDTH), F32)
    for i in range(3):
        turned = jnp.concatenate(
            [grad_recv[head, i * 48 : i * 48 + 48, :].astype(F32)[0:40] for head in range(16)], axis=0
        )
        d_normed = d_normed + dot(jnp.transpose(turned).astype(BF16), w_full[1 + i], NT)
    scaled = d_normed * gain[...]
    d_layer = rstd * (
        scaled
        - jnp.mean(scaled, axis=-1, keepdims=True)
        - normed * jnp.mean(scaled * normed, axis=-1, keepdims=True)
    )
    d2_buf[...] = (
        (up[...].reshape(128, WIDTH).astype(F32) + d_layer) * gelu_slope(pre_two)
    ).astype(BF16)
    row_up = remote(d2_buf.at[pl.ds(112, 16), :], halo2.at[0], hs.at[2], hr.at[2], after)
    row_down = remote(d2_buf.at[pl.ds(0, 16), :], halo2.at[1], hs.at[3], hr.at[3], before)
    row_up.start()
    row_down.start()
    row_up.wait_recv()
    row_down.wait_recv()
    has_before = jnp.where(chip > 0, 1.0, 0.0).astype(BF16)
    has_after = jnp.where(chip < 15, 1.0, 0.0).astype(BF16)
    rows = jnp.concatenate([halo2[0] * has_before, d2_buf[...], halo2[1] * has_after], axis=0)
    tap0, tap1, tap2 = (dot(rows, w_full[4 + i], NT) for i in range(3))
    even_slope = jnp.concatenate([slope1[i, pl.ds(16, 136, stride=2), :] for i in range(5)], axis=1)
    odd_slope = jnp.concatenate([slope1[i, pl.ds(1, 136, stride=2), :] for i in range(5)], axis=1)
    spot = lax.broadcasted_iota(jnp.int32, (136, 1), 0)
    even = tap1[16:152] * even_slope
    even = jnp.where((spot < 128) | (chip < 15), even, 0.0).astype(BF16)
    odd = (tap2[8:144] + tap0[9:145]) * odd_slope
    odd = jnp.where((spot >= 8) | (chip > 0), odd, 0.0).astype(BF16)
    even_mel = dot(even, w_last[...], NT)
    odd_mel = dot(odd, w_last[...], NT)
    mel_even = odd_mel[8:136, 0:128] + even_mel[0:128, 128:256] + odd_mel[7:135, 256:384]
    mel_odd = even_mel[1:129, 0:128] + odd_mel[8:136, 128:256] + even_mel[0:128, 256:384]
    for block in range(2):
        mel_buf[block, 0:64, :] = mel_even[block * 64 : block * 64 + 64]
        mel_buf[block, 64:128, :] = mel_odd[block * 64 : block * 64 + 64]
    swap4 = remote(mel_buf.at[other], mel_recv, xs.at[3], xr.at[3], sibling)
    swap4.start()
    out[core] = mel_buf[core]
    swap4.wait_recv()
    out[other] = mel_recv[...]

    @pl.when(wp_sends)
    def _():
        def body(step, carry):
            wpz(step, z // 4).wait_send()
            return carry

        lax.fori_loop(1, 16, body, 0)

    @pl.when(wr_sends)
    def _():
        def body(step, carry):
            wrz(step, z // 8).wait_send()
            return carry

        lax.fori_loop(1, 16, body, 0)

    for step in range(1, 4):
        for copy in (wp1, wp2, wpc, wr1, wr2, wrc):
            copy(step).wait_send()
    wpc(0).wait_send()
    wrc(0).wait_send()

    def sent(step, carry):
        for copy in (qkv_copy, u_copy, d_copy, b_copy):
            copy(step).wait_send()
        return carry

    lax.fori_loop(1, 16, sent, 0)
    for copy in (swap1, swap2, swap3, swap4, edge_up, edge_down, row_up, row_down):
        copy.wait_send()


def per_device(
    frame_counts, dest_rank, grad_rows, queries, key_rows, value_rows, conv2_pre, conv1_pre,
    norm_gain, w_proj, w_out, w_qkv, w_conv2, w_conv1,
):
    chip_tab, near_tab = tables()
    target = jnp.transpose(dest_rank[0, :, :, 0])
    grads = jnp.transpose(grad_rows[0], (1, 0, 2)).reshape(192, HID)
    anywhere = pl.BlockSpec(memory_space=pl.ANY)
    vmem = pl.BlockSpec(memory_space=pltpu.VMEM)
    scratch = [
        ((192, HID), BF16), ((64, 2, WIDTH), BF16), ((64, 2, WIDTH), BF16), ((64, 2, WIDTH), BF16),
        ((64, 2, WIDTH), BF16), ((128, 2, WIDTH), BF16), ((40, WIDTH), BF16), ((3, 40, WIDTH), BF16),
        ((3, 40, WIDTH), BF16), ((3, 8, WIDTH), BF16), ((2, 128, WIDTH), F32),
        ((320, WIDTH), BF16), ((WIDTH, HID), BF16), ((16, 320, WIDTH), BF16), ((7, WIDTH, WIDTH), BF16),
        ((384, WIDTH), BF16),
        ((2, 192, WIDTH), BF16), ((2, 192, WIDTH), BF16), ((2, 192, WIDTH), BF16), ((2, 192, WIDTH), BF16),
        ((16, 144, 128), BF16), ((144, LENGTH), BF16), ((LENGTH, 48), BF16), ((LENGTH, 48), BF16),
        ((LENGTH, 48), BF16),
        ((16, 16, WIDTH), BF16), ((16, 16, WIDTH), BF16), ((2, 64, WIDTH), BF16), ((2, 64, WIDTH), BF16),
        ((16, 48, 128), BF16), ((48, LENGTH), BF16), ((LENGTH, 48), BF16),
        ((LENGTH, LENGTH), BF16), ((LENGTH, QB), F32), ((1, LENGTH), F32), ((LENGTH, 48), F32),
        ((LENGTH, 48), F32), ((144, LENGTH), BF16), ((16, 144, 128), BF16),
        ((5, 288, 128), F32), ((2, 16, WIDTH), BF16), ((128, WIDTH), BF16), ((2, 16, WIDTH), BF16),
        ((2, 128, 128), F32), ((128, 128), F32),
    ]
    sems = [20, 16, 4, 4, 4, 4, 4, 4, 4, 16, 2, 4, 4, 4, 4, 4, 4, 4, 4, 16, 16, 16, 16, 16, 16, 16, 16, 4, 4]
    result = pl.pallas_call(
        kernel,
        out_shape=jax.ShapeDtypeStruct((2, 128, 128), F32),
        in_specs=[pl.BlockSpec(memory_space=pltpu.SMEM), vmem]
        + [anywhere] * 6 + [vmem] + [anywhere] * 5 + [vmem, anywhere],
        out_specs=vmem,
        scratch_shapes=[pltpu.VMEM(shape, kind) for shape, kind in scratch]
        + [pltpu.SemaphoreType.DMA((n,)) for n in sems],
        compiler_params=pltpu.CompilerParams(
            collective_id=0, has_side_effects=True, vmem_limit_bytes=58 << 20
        ),
    )(
        frame_counts, target, grads, queries, key_rows, value_rows, conv2_pre, conv1_pre,
        norm_gain.reshape(1, WIDTH), w_proj, w_out, w_qkv, w_conv2, w_conv1,
        jnp.asarray(chip_tab), jnp.asarray(near_tab),
    )
    mel = result.reshape(2, 2, 64, 128)
    return jnp.transpose(mel, (2, 1, 0, 3)).reshape(1, 128, 2, 128)


def solution(mesh):
    rows = P("llm", "enc", None, None)
    placed = (
        P("llm", None), rows, P("llm", None, "enc", None), rows, rows, rows, rows, rows, P(),
        P(None, "llm"), P("llm", None), P(None, "llm", None), P(None, "llm", None), P(None, "llm", None),
    )
    return jax.shard_map(
        per_device, mesh=mesh, in_specs=placed, out_specs=rows, check_vma=False
    )
```

time: 327 us -> 120 us (0.37)
  Pallas kernels: 0 us -> 117 us
  blocking collectives: 102 us -> 0 us
  starting transfers between devices: 68.8 us -> 0 us
  waiting for transfers between devices: 42.7 us -> 0 us
  local copies, waits for them, and re-layouts: 45.4 us -> 2.93 us
  matrix products: 35.1 us -> 0 us
  other arithmetic: 16 us -> 0 us
  between operations: 14 us -> 0.01 us
    pallas_call x0 -> x1, Pallas kernels: none -> 117 us  [per_device(): pl.pallas_call(kernel, out_shape=jax.ShapeDtypeStruct((2, 128, 128), F32)...]
    all_gather x2 -> x0, blocking collectives: 102 us -> none  [the longest x1 74.6 us: per_device(): lax.all_gather(w_out, 'llm', axis=0, tiled=True)]
    all_to_all x9 -> x0, starting transfers between devices: 58.9 us -> none  [the longest x1 13 us: per_device(): lax.all_to_all(grad_rows, 'llm', split_axis=1, concat_axis=0, tiled=True)]
    all_to_all x9 -> x0, waiting for transfers between devices: 37.5 us -> none  [the longest x1 7.53 us: per_device(): lax.all_to_all(d_out, 'enc', split_axis=1, concat_axis=0, tiled=True)]
    dot_general x30 -> x0, matrix products: 35.1 us -> none  [the longest x4 6.54 us: step(): jnp.einsum('qnd,knd->nqk', query_part, keyed, preferred_element_type=jnp....]
    unnamed x50 -> x0, local copies, waits for them, and re-layouts: 20.4 us -> none
    ppermute x2 -> x0, starting transfers between devices: 9.84 us -> none  [the longest x1 7.92 us: padded(): lax.ppermute(tail, axis, [(i, (i + 1) % count) for i in range(ends)])]
    all_to_all x19 -> x0, local copies, waits for them, and re-layouts: 6.42 us -> none  [the longest x3 1.83 us: per_device(): lax.all_to_all(grads[1], 'enc', split_axis=0, concat_axis=1, tiled=True)]
  transfers between devices with their start and end apart: 14 -> 0, of which waited for: 8 -> 0; matrix products, arithmetic and copies ran while one was open for 25% -> 0% of each run, Pallas kernels for 0% -> 0%
where the time goes in v1:
time: 120 us
  Pallas kernels  117 us (98%)
  local copies, waits for them, and re-layouts  2.93 us (2%)
    pallas_call x1, Pallas kernels, per_device(): pl.pallas_call(kernel, out_shape=jax.ShapeDtypeStruct((2, 128, 128), F32)...  117 us

profile of v1, /device:TPU:1, one launch (start us, length us, event | category | flops | bytes accessed | tf_op | source)
XLA Modules:
  0.0 120.2 jit_solution(7285922297563804570)
XLA Ops:
  0.0 1.3 %reshape.13.gain = f32[1,640]{1,0:T(1,128)} reshape(f32[640]{0:T(1024)} %param.24) | data formatting | bytes 5120 | tf_op jit(solution)/shard_map/reshape | solution.py:619
  1.3 117.2 %shard_map.154 = f32[2,128,128]{2,1,0:T(8,128)} custom-call(s32[1,2]{1,0:T(1,128)} %counts.1, s32[2,64]{1,0:T(2,128)} %bitcast.14, bf16[192,2048]{1,0:T(8,128)(2,1)} %bitcast.12, bf16[1,64,2,640]{3,2,1,0:T(2,128)(2,1)} %q_in.1, bf16[1,64,2,640]{3,2,1,0:T(2,128)(2,1)} %k_in.1, bf16[1,64,2,640]{3,2,1,0:T(2,128)(2,1)} %v_in.1, bf16[1,64,2,640]{3,2,1,0:T(2,128)(2,1)} %c2_in.1, ...), custom_call_target="tpu_custom_call" | custom-call | tf_op jit(solution)/shard_map/pallas_call | solution.py:606
  118.5 1.7 %copy.17 = f32[64,2,2,128]{3,2,1,0:T(2,128)} copy(f32[64,2,2,128]{3,0,1,2:T(8,128)} %bitcast.13) | data formatting | bytes 262144 | tf_op jit(solution)/shard_map/transpose | solution.py:623

commit v2 on v1

v2 whole, which is shorter than its diff:
```python
import functools

import jax
import jax.numpy as jnp
import numpy as np
from jax import lax
from jax.experimental import pallas as pl
from jax.experimental.pallas import tpu as pltpu
from jax.sharding import PartitionSpec as P

MESH = pl.DeviceIdType.MESH
F32, BF16 = jnp.float32, jnp.bfloat16
HEAD_DIM = 40
WIDTH = 640
HID = 2048
LENGTH = 2048
SCALE = HEAD_DIM ** (-0.5)
LOG2E = 1.4426950408889634
MASKED = -1e30
ROOT_HALF = 0.7071067811865476
INV_ROOT_TWO_PI = 0.3989422804014327
QB = 512


def gelu_value(value):
    return value * 0.5 * (1.0 + lax.erf(value * ROOT_HALF))


def gelu_slope(value):
    return (
        0.5 * (1.0 + lax.erf(value * ROOT_HALF))
        + value * jnp.exp(-0.5 * value * value) * INV_ROOT_TWO_PI
    )


def dot(a, b, dims):
    return lax.dot_general(a, b, (dims, ((), ())), preferred_element_type=F32)


NN = ((1,), (0,))
NT = ((1,), (1,))
TN = ((0,), (0,))


def tables():
    inverse = 10000.0 ** (-np.arange(320) / 319.0)
    base = 128.0 * np.arange(16)[:, None] * inverse[None, :]
    local = np.arange(128.0)[:, None] * inverse[None, :]
    first = np.concatenate([np.sin(base), np.cos(base)], axis=1)
    second = np.concatenate([np.cos(base), -np.sin(base)], axis=1)
    chip = np.stack([first, second], axis=1).astype(np.float32)
    near = np.stack(
        [np.concatenate([np.cos(local)] * 2, 1), np.concatenate([np.sin(local)] * 2, 1)]
    ).astype(np.float32)
    return chip, near


def kernel(
    counts, target_in, grads, q_in, k_in, v_in, c2_in, c1_in, gain_in, wp_in, wo_in, wqkv_in, wc2_in, wc1_in,
    chip_tab, near_tab,
    out,
    target, gain, pair, g_loc, q_loc, k_loc, v_loc, c2_loc, c1_loc, wo_loc, wqkv_loc, wc2_loc, wc1_loc, near,
    a_slab, b_slab, wp, wa, wb, w_full, w_last,
    cl1, cl2, xb1, xb2, head_send, qkv, qt, kt, vt, kn, vn, qn,
    u_send, u_recv, up_send, up, d_send, d_out, dn,
    e_mat, big, rl, delta, attn, dk_acc, dv_acc, dq_t, dkv_t, dq_recv, dkv_recv,
    slope1, halo1, d2_buf, halo2, mel_buf, mel_recv,
    loc_sem, wpz_s, wpz_r, wp1_s, wp1_r, wp2_s, wp2_r, wpc_s, wpc_r,
    waz_s, waz_r, wa1_s, wa1_r, wa2_s, wa2_r, wac_s, wac_r,
    wbz_s, wbz_r, wb1_s, wb1_r, wb2_s, wb2_r, wbc_s, wbc_r,
    xs, xr, qs, qr, us, ur, ds_, dr, bs, br, cs, cr, hs, hr,
):
    z = lax.axis_index("llm")
    e = lax.axis_index("enc")
    core = lax.rem(e, 2)
    other = 1 - core
    chip = e // 2
    x = lax.rem(chip, 4)
    y = chip // 4
    a = jnp.where(core == 0, x, y)
    b = jnp.where(core == 0, y, x)
    sibling = (z, chip * 2 + other)

    def along_a(step):
        to = lax.rem(a + step, 4)
        return (z, jnp.where(core == 0, y * 4 + to, to * 4 + x) * 2 + core)

    def along_b(step):
        to = lax.rem(b + step, 4)
        return (z, jnp.where(core == 0, to * 4 + x, y * 4 + to) * 2 + core)

    def along_z(step):
        return (lax.rem(z + step, 16), e)

    def on_chip(number):
        return (z, number * 2 + core)

    def remote(src, dst, send, recv, device):
        return pltpu.make_async_remote_copy(
            src_ref=src, dst_ref=dst, send_sem=send, recv_sem=recv, device_id=device, device_id_type=MESH
        )

    def each(low, high, act):
        def body(step, carry):
            act(step)
            return carry

        lax.fori_loop(low, high, body, 0)

    barrier = pltpu.get_barrier_semaphore()

    def greet(step):
        pl.semaphore_signal(barrier, inc=1, device_id=along_z(step), device_id_type=MESH)
        pl.semaphore_signal(
            barrier, inc=1, device_id=on_chip(lax.rem(chip + step, 16)), device_id_type=MESH
        )

    each(1, 16, greet)
    pl.semaphore_signal(barrier, inc=1, device_id=sibling, device_id_type=MESH)

    loads = [
        (q_in.at[0], q_loc), (k_in.at[0], k_loc), (v_in.at[0], v_loc), (wo_in, wo_loc), (wc1_in, wc1_loc),
        (wqkv_in, wqkv_loc), (wc2_in, wc2_loc), (c2_in.at[0], c2_loc), (c1_in.at[0], c1_loc),
        (grads, g_loc), (near_tab, near), (target_in, target), (gain_in, gain), (chip_tab.at[chip], pair),
    ]
    for i, (src, dst) in enumerate(loads):
        pltpu.make_async_copy(src, dst, loc_sem.at[i]).start()

    def loaded(i):
        pltpu.make_async_copy(loads[i][0], loads[i][1], loc_sem.at[i]).wait()

    pl.semaphore_wait(barrier, 31)

    piece = 2 * b + a // 2
    kind = lax.rem(a, 2) + 2 * core
    wp_rows = pl.ds(pl.multiple_of(piece * 80, 16), 80)

    def wpz(step, index):
        return remote(
            wp_in.at[wp_rows, :],
            wp.at[wp_rows, pl.ds(pl.multiple_of((kind * 4 + index) * 128, 128), 128)],
            wpz_s.at[step], wpz_r.at[index], along_z(step),
        )

    wp_sends = lax.rem(z, 4) == kind
    wp_own = pltpu.make_async_copy(
        wp_in.at[wp_rows, :],
        wp.at[wp_rows, pl.ds(pl.multiple_of((kind * 4 + z // 4) * 128, 128), 128)],
        loc_sem.at[14],
    )

    @pl.when(wp_sends)
    def _():
        each(1, 16, lambda step: wpz(step, z // 4).start())
        wp_own.start()

    for i, ref in enumerate((q_loc, k_loc, v_loc)):
        loaded(i)
        for clip in range(2):
            cl1[clip, i * 64 : (i + 1) * 64, :] = ref[:, clip, :]
    swap1 = remote(cl1.at[other], xb1.at[core], xs.at[0], xr.at[0], sibling)
    swap1.start()
    keep1 = pltpu.make_async_copy(cl1.at[core], xb1.at[core], loc_sem.at[15])
    keep1.start()

    swap1.wait_recv()
    keep1.wait()
    zero_rows = jnp.zeros((8, 128), F32)
    turned = []
    for i in range(3):
        rows = jnp.concatenate(
            [xb1[0, i * 64 : (i + 1) * 64, :], xb1[1, i * 64 : (i + 1) * 64, :]], axis=0
        ).astype(F32)
        turned.append(jnp.transpose(rows))
    for head in range(16):
        head_send[head] = jnp.concatenate(
            [part[head * 40 : head * 40 + 40] for part in turned] + [zero_rows], axis=0
        ).astype(BF16)
    chip_lanes = pl.ds(pl.multiple_of(chip * 128, 128), 128)

    def qkv_copy(step):
        to = lax.rem(chip + step, 16)
        return remote(head_send.at[to], qkv.at[:, chip_lanes], qs.at[step], qr.at[step], on_chip(to))

    each(1, 16, lambda step: qkv_copy(step).start())
    qkv_own = pltpu.make_async_copy(head_send.at[chip], qkv.at[:, chip_lanes], loc_sem.at[18])
    qkv_own.start()

    for index in range(4):
        @pl.when(kind + 4 * index != z)
        def _():
            wpz(1, index).wait_recv()

    @pl.when(wp_sends)
    def _():
        wp_own.wait()

    def wp1(step):
        block = wp.at[wp_rows, pl.ds(pl.multiple_of(kind * 512, 128), 512)]
        return remote(block, block, wp1_s.at[step], wp1_r.at[step], along_a(step))

    for step in range(1, 4):
        wp1(step).start()

    group8 = a + 4 * core

    class Slab:
        def __init__(self, rows, held, full, sems, own_sem):
            self.rows, self.held, self.full = rows, held, full
            self.zs, self.zr, self.s1, self.r1, self.s2, self.r2, self.s3, self.r3 = sems
            self.part = pl.ds(pl.multiple_of(b * rows, 16), rows)
            self.sends = lax.rem(z, 8) == group8
            self.own = pltpu.make_async_copy(
                held.at[self.part, :], full.at[group8 * 2 + z // 8, self.part, :], own_sem
            )

        def deep(self, step, index):
            return remote(
                self.held.at[self.part, :], self.full.at[group8 * 2 + index, self.part, :],
                self.zs.at[step], self.zr.at[index], along_z(step),
            )

        def start_deep(self):
            @pl.when(self.sends)
            def _():
                each(1, 16, lambda step: self.deep(step, z // 8).start())
                self.own.start()

        def wait_deep(self):
            for index in range(2):
                @pl.when(group8 + 8 * index != z)
                def _():
                    self.deep(1, index).wait_recv()

            @pl.when(self.sends)
            def _():
                self.own.wait()

        def one(self, step):
            block = self.full.at[pl.ds(group8 * 2, 2), self.part, :]
            return remote(block, block, self.s1.at[step], self.r1.at[step], along_a(step))

        def band(self, number):
            return self.full.at[
                pl.ds(core * 8, 8), pl.ds(pl.multiple_of(number * self.rows, 16), self.rows), :
            ]

        def two(self, step):
            return remote(self.band(b), self.band(b), self.s2.at[step], self.r2.at[step], along_b(step))

        def cross(self, step):
            band = self.band(lax.rem(b - step + 4, 4))
            return remote(band, band, self.s3.at[step], self.r3.at[step], sibling)

        def sent(self):
            @pl.when(self.sends)
            def _():
                each(1, 16, lambda step: self.deep(step, z // 8).wait_send())

            for step in range(1, 4):
                self.one(step).wait_send()
                self.two(step).wait_send()
            for step in range(4):
                self.cross(step).wait_send()

    slab_a = Slab(
        16, a_slab, wa, (waz_s, waz_r, wa1_s, wa1_r, wa2_s, wa2_r, wac_s, wac_r), loc_sem.at[16]
    )
    slab_b = Slab(
        64, b_slab, wb, (wbz_s, wbz_r, wb1_s, wb1_r, wb2_s, wb2_r, wbc_s, wbc_r), loc_sem.at[17]
    )
    loaded(3)
    loaded(4)
    parts = [wo_loc[...].astype(F32)] + [wc1_loc[i].astype(F32) for i in range(3)]
    a_slab[...] = jnp.concatenate(parts, axis=0).astype(BF16)
    slab_a.start_deep()
    loaded(5)
    loaded(6)
    parts = [wqkv_loc[i].astype(F32) for i in range(3)] + [wc2_loc[i].astype(F32) for i in range(3)]
    b_slab[...] = jnp.concatenate(parts + [jnp.zeros((16, WIDTH), F32)], axis=0).astype(BF16)
    slab_b.start_deep()

    for step in range(1, 4):
        wp1(step).wait_recv()

    def wp_set(number):
        return wp.at[
            pl.ds(pl.multiple_of(number * 160, 16), 160), pl.ds(pl.multiple_of(core * 1024, 128), 1024)
        ]

    def wp2(step):
        return remote(wp_set(b), wp_set(b), wp2_s.at[step], wp2_r.at[step], along_b(step))

    def wpc(step):
        held = wp_set(lax.rem(b - step + 4, 4))
        return remote(held, held, wpc_s.at[step], wpc_r.at[step], sibling)

    for step in (2, 1, 3):
        wp2(step).start()
    wpc(0).start()

    for step in (1, 3, 2):
        wp2(step).wait_recv()
        wpc(step).start()

    slab_a.wait_deep()
    for step in range(1, 4):
        slab_a.one(step).start()
    slab_b.wait_deep()
    for step in range(1, 4):
        slab_b.one(step).start()

    loaded(9)
    for step in range(4):
        wpc(step).wait_recv()

    total = jnp.zeros((192, WIDTH), F32)
    for number in range(4):
        rows = jnp.concatenate(
            [g_loc[:, (number + 4 * i) * 128 : (number + 4 * i + 1) * 128] for i in range(4)], axis=1
        )
        total = total + dot(rows, wp[:, number * 512 : (number + 1) * 512], NT)
    slot_row = lax.broadcasted_iota(jnp.int32, (256, 192), 0)
    held_row = lax.broadcasted_iota(jnp.int32, (256, 192), 1)
    order = (lax.rem(slot_row, 16) * 16 + slot_row // 16 == held_row).astype(F32).astype(BF16)
    u_send[...] = dot(order, total.astype(BF16), NN).astype(BF16).reshape(16, 16, WIDTH)

    def u_copy(step):
        to = lax.rem(z + step, 16)
        return remote(u_send.at[to], u_recv.at[z], us.at[step], ur.at[step], (to, e))

    each(1, 16, lambda step: u_copy(step).start())
    u_own = pltpu.make_async_copy(u_send.at[z], u_recv.at[z], loc_sem.at[19])
    u_own.start()

    loaded(7)
    loaded(8)
    for clip in range(2):
        cl2[clip, 0:64, :] = c2_loc[:, clip, :]
        cl2[clip, 64:192, :] = c1_loc[:, clip, :]
    swap2 = remote(cl2.at[other], xb2.at[core], xs.at[1], xr.at[1], sibling)
    swap2.start()
    keep2 = pltpu.make_async_copy(cl2.at[core], xb2.at[core], loc_sem.at[20])
    keep2.start()

    for slab in (slab_a, slab_b):
        for step in range(1, 4):
            slab.one(step).wait_recv()
        for step in (2, 1, 3):
            slab.two(step).start()
        slab.cross(0).start()

    swap2.wait_recv()
    keep2.wait()
    after = on_chip(lax.rem(chip + 1, 16))
    before = on_chip(lax.rem(chip + 15, 16))
    edge_up = remote(xb2.at[1, pl.ds(176, 16), :], halo1.at[0], hs.at[0], hr.at[0], after)
    edge_down = remote(xb2.at[0, pl.ds(64, 16), :], halo1.at[1], hs.at[1], hr.at[1], before)
    edge_up.start()
    edge_down.start()

    each(1, 16, lambda step: qkv_copy(step).wait_recv())
    qkv_own.wait()
    row8 = lax.broadcasted_iota(jnp.int32, (8, LENGTH), 0)
    places = lax.broadcasted_iota(jnp.int32, (8, LENGTH), 1)
    own_count = jnp.where(core == 0, counts[0, 0], counts[0, 1])
    ones_rows = jnp.where(row8 == 0, 1.0, 0.0)
    bias_rows = jnp.where((row8 == 0) & (places >= own_count), MASKED, 0.0)
    arrived = qkv[...].astype(F32)
    wide_q = jnp.concatenate([arrived[0:40], ones_rows], axis=0)
    wide_k = jnp.concatenate([arrived[40:80], bias_rows], axis=0)
    wide_v = arrived[80:128]
    qt[...] = wide_q.astype(BF16)
    kt[...] = wide_k.astype(BF16)
    vt[...] = wide_v.astype(BF16)
    qn[...] = jnp.transpose(wide_q).astype(BF16)
    kn[...] = jnp.transpose(wide_k).astype(BF16)
    vn[...] = jnp.transpose(wide_v).astype(BF16)

    def exponentials(number):
        lanes = pl.ds(pl.multiple_of(number * QB, QB), QB)
        big[...] = dot(kn[...], qt[:, lanes], NN)
        highest = jnp.max(big[...], axis=0, keepdims=True)
        weights = jnp.exp2((big[...] - highest) * (SCALE * LOG2E))
        weights_b = weights.astype(BF16)
        e_mat[:, lanes] = weights_b
        share = 1.0 / jnp.sum(weights, axis=0, keepdims=True)
        rl[:, lanes] = share
        attn[:, lanes] = dot(vt[...], weights_b, NN) * share

    each(0, LENGTH // QB, exponentials)

    for step in (1, 3, 2):
        slab_a.two(step).wait_recv()
        slab_a.cross(step).start()
    for step in range(4):
        slab_a.cross(step).wait_recv()

    def slabs_of(full, number):
        return [full[lax.rem(place, 8) * 2 + place // 8].astype(F32) for place in (2 * number, 2 * number + 1)]

    def compact_a(number):
        slabs = slabs_of(wa, number)
        rows = pl.ds(pl.multiple_of(number * 80, 16), 80)
        w_full[0, rows, :] = jnp.concatenate([slab[0:40] for slab in slabs], axis=0).astype(BF16)
        for i in range(3):
            w_last[pl.ds(pl.multiple_of(i * 128 + number * 16, 16), 16), :] = jnp.concatenate(
                [slab[40 + i * 8 : 48 + i * 8] for slab in slabs], axis=0
            ).astype(BF16)

    each(0, 8, compact_a)

    loaded(11)
    slots = lax.broadcasted_iota(jnp.int32, (256, 64), 0)
    frame = e * 64 + lax.broadcasted_iota(jnp.int32, (256, 64), 1)
    named = []
    for clip in range(2):
        hit = (target[clip : clip + 1, :] == slots // 16) & (frame < counts[0, clip])
        named.append(jnp.where(hit, 1.0, 0.0))
    earlier = lax.broadcasted_iota(jnp.int32, (64, 64), 0)
    later = lax.broadcasted_iota(jnp.int32, (64, 64), 1)
    upto = (earlier <= later).astype(F32).astype(BF16)
    under = (earlier < later).astype(F32).astype(BF16)
    named_b = [part.astype(BF16) for part in named]
    seen = [
        dot(named_b[0], upto, NN) + dot(named_b[1], under, NN),
        dot(named_b[0], upto, NN) + dot(named_b[1], upto, NN),
    ]
    within = lax.rem(slots, 16).astype(F32) + 1.0
    choose = jnp.transpose(
        jnp.concatenate([jnp.where(seen[i] == within, named[i], 0.0) for i in range(2)], axis=1)
    ).astype(BF16)

    each(1, 16, lambda step: u_copy(step).wait_recv())
    u_own.wait()
    up_send[...] = (
        dot(choose, u_recv[...].reshape(256, WIDTH), NN).astype(BF16).reshape(2, 64, WIDTH)
    )
    swap3 = remote(up_send.at[other], up.at[core], xs.at[2], xr.at[2], sibling)
    swap3.start()
    keep3 = pltpu.make_async_copy(up_send.at[core], up.at[core], loc_sem.at[21])
    keep3.start()
    swap3.wait_recv()
    keep3.wait()
    d_attn = dot(w_full[0], up[...].reshape(128, WIDTH), NT)
    for head in range(16):
        d_send[head] = jnp.concatenate([d_attn[head * 40 : head * 40 + 40], zero_rows], axis=0).astype(
            BF16
        )

    def d_copy(step):
        to = lax.rem(chip + step, 16)
        return remote(d_send.at[to], d_out.at[:, chip_lanes], ds_.at[step], dr.at[step], on_chip(to))

    each(1, 16, lambda step: d_copy(step).start())
    d_own = pltpu.make_async_copy(d_send.at[chip], d_out.at[:, chip_lanes], loc_sem.at[22])
    d_own.start()

    edge_up.wait_recv()
    edge_down.wait_recv()
    for i in range(5):
        lanes = slice(i * 128, i * 128 + 128)
        slope1[i, 0:16, :] = gelu_slope(halo1[0, :, lanes].astype(F32))
        slope1[i, 16:144, :] = gelu_slope(xb2[0, 64:192, lanes].astype(F32))
        slope1[i, 144:272, :] = gelu_slope(xb2[1, 64:192, lanes].astype(F32))
        slope1[i, 272:288, :] = gelu_slope(halo1[1, :, lanes].astype(F32))

    each(1, 16, lambda step: d_copy(step).wait_recv())
    d_own.wait()
    shared = d_out[...].astype(F32) * rl[...]
    d_out[...] = shared.astype(BF16)
    dn[...] = jnp.transpose(shared).astype(BF16)
    delta[...] = jnp.sum(shared * attn[...], axis=0, keepdims=True)
    dk_acc[...] = jnp.zeros_like(dk_acc)
    dv_acc[...] = jnp.zeros_like(dv_acc)

    def place_lanes(ref, number):
        return ref.at[:, pl.ds(pl.multiple_of(number * 128, 128), 128)]

    def b_copy(step):
        to = lax.rem(chip + step, 16)
        return remote(place_lanes(dq_t, to), dq_recv.at[chip], bs.at[step], br.at[step], on_chip(to))

    def gradients(number):
        block = lax.rem(chip // (QB // 128) + number, LENGTH // QB)
        lanes = pl.ds(pl.multiple_of(block * QB, QB), QB)
        weights = e_mat[:, lanes]
        moved = dot(vn[...], d_out[:, lanes], NN) - delta[:, lanes]
        slopes = (weights.astype(F32) * moved).astype(BF16)
        dq_t[:, lanes] = (dot(kt[...], slopes, NN) * SCALE).astype(BF16)
        for part in range(QB // 128):
            step = lax.rem(QB // 128 * block + part - chip + 16, 16)

            @pl.when(step > 0)
            def _():
                b_copy(step).start()

        dv_acc[...] += dot(weights, dn[lanes, :], NN)
        dk_acc[...] += dot(slopes, qn[lanes, :], NN)

    each(0, LENGTH // QB, gradients)
    turned = jnp.transpose(dk_acc[...] * SCALE)[0:40]
    dkv_t[...] = jnp.concatenate([turned, jnp.transpose(dv_acc[...])[0:40]], axis=0).astype(BF16)

    def c_copy(step):
        to = lax.rem(chip + step, 16)
        return remote(place_lanes(dkv_t, to), dkv_recv.at[chip], cs.at[step], cr.at[step], on_chip(to))

    each(1, 16, lambda step: c_copy(step).start())
    b_own = pltpu.make_async_copy(place_lanes(dq_t, chip), dq_recv.at[chip], loc_sem.at[23])
    c_own = pltpu.make_async_copy(place_lanes(dkv_t, chip), dkv_recv.at[chip], loc_sem.at[24])
    b_own.start()
    c_own.start()

    for step in (1, 3, 2):
        slab_b.two(step).wait_recv()
        slab_b.cross(step).start()

    loaded(10)
    loaded(12)
    loaded(13)
    pre_two = jnp.concatenate([xb2[0, 0:64, :], xb2[1, 0:64, :]], axis=0).astype(F32)
    slope2 = gelu_slope(pre_two)
    layer_in = gelu_value(pre_two) + pair[0:1] * near[0] + pair[1:2] * near[1]
    center = jnp.mean(layer_in, axis=-1, keepdims=True)
    moved = layer_in - center
    rstd = 1.0 / jnp.sqrt(jnp.mean(moved * moved, axis=-1, keepdims=True) + 1e-05)
    normed = moved * rstd

    for step in range(4):
        slab_b.cross(step).wait_recv()

    def compact_b(number):
        slabs = slabs_of(wb, number)
        rows = pl.ds(pl.multiple_of(number * 80, 16), 80)
        for i in range(6):
            w_full[1 + i, rows, :] = jnp.concatenate(
                [slab[i * 40 : i * 40 + 40] for slab in slabs], axis=0
            ).astype(BF16)

    each(0, 8, compact_b)

    @pl.when(wp_sends)
    def _():
        each(1, 16, lambda step: wpz(step, z // 4).wait_send())

    for step in range(1, 4):
        for copy in (wp1, wp2, wpc):
            copy(step).wait_send()
    wpc(0).wait_send()
    slab_a.sent()
    slab_b.sent()

    def sent(step):
        for copy in (qkv_copy, u_copy, d_copy, b_copy):
            copy(step).wait_send()

    each(1, 16, sent)
    for copy in (swap1, swap2, swap3, edge_up, edge_down):
        copy.wait_send()

    each(1, 16, lambda step: b_copy(step).wait_recv())
    b_own.wait()
    c_own.wait()
    each(1, 16, lambda step: c_copy(step).wait_recv())
    d_normed = jnp.zeros((128, WIDTH), F32)
    for i, (ref, low) in enumerate(((dq_recv, 0), (dkv_recv, 0), (dkv_recv, 40))):
        turned = jnp.concatenate([ref[head].astype(F32)[low : low + 40] for head in range(16)], axis=0)
        d_normed = d_normed + dot(jnp.transpose(turned).astype(BF16), w_full[1 + i], NT)
    scaled = d_normed * gain[...].reshape(1, WIDTH)
    d_layer = rstd * (
        scaled
        - jnp.mean(scaled, axis=-1, keepdims=True)
        - normed * jnp.mean(scaled * normed, axis=-1, keepdims=True)
    )
    d2_buf[...] = ((up[...].reshape(128, WIDTH).astype(F32) + d_layer) * slope2).astype(BF16)
    row_up = remote(d2_buf.at[pl.ds(112, 16), :], halo2.at[0], hs.at[2], hr.at[2], after)
    row_down = remote(d2_buf.at[pl.ds(0, 16), :], halo2.at[1], hs.at[3], hr.at[3], before)
    row_up.start()
    row_down.start()
    each(1, 16, lambda step: c_copy(step).wait_send())
    row_up.wait_recv()
    row_down.wait_recv()
    has_before = jnp.where(chip > 0, 1.0, 0.0).astype(BF16)
    has_after = jnp.where(chip < 15, 1.0, 0.0).astype(BF16)
    rows = jnp.concatenate([halo2[0] * has_before, d2_buf[...], halo2[1] * has_after], axis=0)
    tap0, tap1, tap2 = (dot(rows, w_full[4 + i], NT) for i in range(3))
    even_slope = jnp.concatenate([slope1[i, pl.ds(16, 136, stride=2), :] for i in range(5)], axis=1)
    odd_slope = jnp.concatenate([slope1[i, pl.ds(1, 136, stride=2), :] for i in range(5)], axis=1)
    spot = lax.broadcasted_iota(jnp.int32, (136, 1), 0)
    even = tap1[16:152] * even_slope
    even = jnp.where((spot < 128) | (chip < 15), even, 0.0).astype(BF16)
    odd = (tap2[8:144] + tap0[9:145]) * odd_slope
    odd = jnp.where((spot >= 8) | (chip > 0), odd, 0.0).astype(BF16)
    even_mel = dot(even, w_last[...], NT)
    odd_mel = dot(odd, w_last[...], NT)
    mel_even = odd_mel[8:136, 0:128] + even_mel[0:128, 128:256] + odd_mel[7:135, 256:384]
    mel_odd = even_mel[1:129, 0:128] + odd_mel[8:136, 128:256] + even_mel[0:128, 256:384]
    for block in range(2):
        mel_buf[block, 0:64, :] = mel_even[block * 64 : block * 64 + 64]
        mel_buf[block, 64:128, :] = mel_odd[block * 64 : block * 64 + 64]
    swap4 = remote(mel_buf.at[other], mel_recv, xs.at[3], xr.at[3], sibling)
    swap4.start()
    for half in range(2):
        own = mel_buf[core, half * 64 : half * 64 + 64, :]
        out[pl.ds(2 * half + core, 64, stride=4), :] = own
    swap4.wait_recv()
    for half in range(2):
        out[pl.ds(2 * half + other, 64, stride=4), :] = mel_recv[half * 64 : half * 64 + 64, :]
    for copy in (swap4, row_up, row_down):
        copy.wait_send()


def per_device(
    frame_counts, dest_rank, grad_rows, queries, key_rows, value_rows, conv2_pre, conv1_pre,
    norm_gain, w_proj, w_out, w_qkv, w_conv2, w_conv1,
):
    chip_tab, near_tab = tables()
    target = jnp.transpose(dest_rank[0, :, :, 0])
    grads = jnp.transpose(grad_rows[0], (1, 0, 2)).reshape(192, HID)
    anywhere = pl.BlockSpec(memory_space=pl.ANY)
    vmem = pl.BlockSpec(memory_space=pltpu.VMEM)
    scratch = [
        ((2, 64), jnp.int32), ((WIDTH,), F32), ((2, WIDTH), F32),
        ((192, HID), BF16), ((64, 2, WIDTH), BF16), ((64, 2, WIDTH), BF16), ((64, 2, WIDTH), BF16),
        ((64, 2, WIDTH), BF16), ((128, 2, WIDTH), BF16), ((40, WIDTH), BF16), ((3, 40, WIDTH), BF16),
        ((3, 40, WIDTH), BF16), ((3, 8, WIDTH), BF16), ((2, 128, WIDTH), F32),
        ((64, WIDTH), BF16), ((256, WIDTH), BF16), ((WIDTH, HID), BF16), ((16, 64, WIDTH), BF16),
        ((16, 256, WIDTH), BF16), ((7, WIDTH, WIDTH), BF16), ((384, WIDTH), BF16),
        ((2, 192, WIDTH), BF16), ((2, 192, WIDTH), BF16), ((2, 192, WIDTH), BF16), ((2, 192, WIDTH), BF16),
        ((16, 128, 128), BF16), ((128, LENGTH), BF16), ((48, LENGTH), BF16), ((48, LENGTH), BF16), ((48, LENGTH), BF16),
        ((LENGTH, 48), BF16), ((LENGTH, 48), BF16), ((LENGTH, 48), BF16),
        ((16, 16, WIDTH), BF16), ((16, 16, WIDTH), BF16), ((2, 64, WIDTH), BF16), ((2, 64, WIDTH), BF16),
        ((16, 48, 128), BF16), ((48, LENGTH), BF16), ((LENGTH, 48), BF16),
        ((LENGTH, LENGTH), BF16), ((LENGTH, QB), F32), ((1, LENGTH), F32), ((1, LENGTH), F32), ((48, LENGTH), F32), ((LENGTH, 48), F32),
        ((LENGTH, 48), F32), ((48, LENGTH), BF16), ((80, LENGTH), BF16), ((16, 48, 128), BF16),
        ((16, 80, 128), BF16),
        ((5, 288, 128), F32), ((2, 16, WIDTH), BF16), ((128, WIDTH), BF16), ((2, 16, WIDTH), BF16),
        ((2, 128, 128), F32), ((128, 128), F32),
    ]
    sems = [25, 16] + [4] * 7 + [16, 2] + [4] * 6 + [16, 2] + [4] * 6 + [4, 4] + [16] * 10 + [4, 4]
    result = pl.pallas_call(
        kernel,
        out_shape=jax.ShapeDtypeStruct((256, 128), F32),
        in_specs=[pl.BlockSpec(memory_space=pltpu.SMEM)] + [anywhere] * 15,
        out_specs=vmem,
        scratch_shapes=[pltpu.VMEM(shape, kind) for shape, kind in scratch]
        + [pltpu.SemaphoreType.DMA((n,)) for n in sems],
        compiler_params=pltpu.CompilerParams(
            collective_id=0, has_side_effects=True, vmem_limit_bytes=58 << 20
        ),
    )(
        frame_counts, target, grads, queries, key_rows, value_rows, conv2_pre, conv1_pre,
        norm_gain, w_proj, w_out, w_qkv, w_conv2, w_conv1,
        jnp.asarray(chip_tab), jnp.asarray(near_tab),
    )
    return result.reshape(1, 128, 2, 128)


def solution(mesh):
    rows = P("llm", "enc", None, None)
    placed = (
        P("llm", None), rows, P("llm", None, "enc", None), rows, rows, rows, rows, rows, P(),
        P(None, "llm"), P("llm", None), P(None, "llm", None), P(None, "llm", None), P(None, "llm", None),
    )
    return jax.shard_map(
        per_device, mesh=mesh, in_specs=placed, out_specs=rows, check_vma=False
    )
```

time: 120 us -> 109 us (0.908)
  Pallas kernels: 117 us -> 107 us
  local copies, waits for them, and re-layouts: 2.93 us -> 1.57 us
    pallas_call x1, Pallas kernels: 117 us -> 107 us  [per_device(): pl.pallas_call(kernel, out_shape=jax.ShapeDtypeStruct((256, 128), F32), i...]
    transpose x1 -> x0, local copies, waits for them, and re-layouts: 1.66 us -> none  [per_device(): return jnp.transpose(mel, (2, 1, 0, 3)).reshape(1, 128, 2, 128)]
    unnamed x0 -> x1, local copies, waits for them, and re-layouts: none -> 1.57 us
    reshape x1 -> x0, local copies, waits for them, and re-layouts: 1.27 us -> none  [per_device(): norm_gain.reshape(1, WIDTH)]
where the time goes in v2:
time: 109 us
  Pallas kernels  107 us (98%)
  local copies, waits for them, and re-layouts  1.57 us (1%)
    pallas_call x1, Pallas kernels, per_device(): pl.pallas_call(kernel, out_shape=jax.ShapeDtypeStruct((256, 128), F32), i...  107 us

profile of v2, /device:TPU:1, one launch (start us, length us, event | category | flops | bytes accessed | tf_op | source)
XLA Modules:
  0.0 108.7 jit_solution(14389720986342197567)
XLA Ops:
  0.0 107.1 %shard_map.154 = f32[256,128]{1,0:T(8,128)} custom-call(s32[1,2]{1,0:T(1,128)} %counts.1, s32[2,64]{1,0:T(2,128)} %bitcast.11, bf16[192,2048]{1,0:T(8,128)(2,1)} %bitcast.9, bf16[1,64,2,640]{3,2,1,0:T(2,128)(2,1)} %q_in.1, bf16[1,64,2,640]{3,2,1,0:T(2,128)(2,1)} %k_in.1, bf16[1,64,2,640]{3,2,1,0:T(2,128)(2,1)} %v_in.1, bf16[1,64,2,640]{3,2,1,0:T(2,128)(2,1)} %c2_in.1, ...), custom_call_target="tpu_custom_call" | custom-call | tf_op jit(solution)/shard_map/pallas_call | solution.py:642
  107.1 1.6 %copy.18 = f32[1,128,2,128]{3,2,1,0:T(2,128)} copy(f32[1,128,2,128]{3,2,1,0:T(2,128)} %bitcast.10) | data formatting | bytes 262144

commit v3 on v2

--- a/solution.py
+++ b/solution.py
@@ -63,12 +63,12 @@
     a_slab, b_slab, wp, wa, wb, w_full, w_last,
     cl1, cl2, xb1, xb2, head_send, qkv, qt, kt, vt, kn, vn, qn,
     u_send, u_recv, up_send, up, d_send, d_out, dn,
-    e_mat, big, rl, delta, attn, dk_acc, dv_acc, dq_t, dkv_t, dq_recv, dkv_recv,
+    e_mat, big, rl, delta, attn, dk_acc, dq_t, dk_t, dv_t, dq_recv, dk_recv, dv_recv,
     slope1, halo1, d2_buf, halo2, mel_buf, mel_recv,
     loc_sem, wpz_s, wpz_r, wp1_s, wp1_r, wp2_s, wp2_r, wpc_s, wpc_r,
     waz_s, waz_r, wa1_s, wa1_r, wa2_s, wa2_r, wac_s, wac_r,
     wbz_s, wbz_r, wb1_s, wb1_r, wb2_s, wb2_r, wbc_s, wbc_r,
-    xs, xr, qs, qr, us, ur, ds_, dr, bs, br, cs, cr, hs, hr,
+    xs, xr, qs, qr, us, ur, ds_, dr, bs, br, cs, cr, vs, vr, hs, hr,
 ):
     z = lax.axis_index("llm")
     e = lax.axis_index("enc")
@@ -306,9 +306,6 @@
     slab_a.wait_deep()
     for step in range(1, 4):
         slab_a.one(step).start()
-    slab_b.wait_deep()
-    for step in range(1, 4):
-        slab_b.one(step).start()
 
     loaded(9)
     for step in range(4):
@@ -343,12 +340,14 @@
     keep2 = pltpu.make_async_copy(cl2.at[core], xb2.at[core], loc_sem.at[20])
     keep2.start()
 
-    for slab in (slab_a, slab_b):
-        for step in range(1, 4):
-            slab.one(step).wait_recv()
-        for step in (2, 1, 3):
-            slab.two(step).start()
-        slab.cross(0).start()
+    for step in range(1, 4):
+        slab_a.one(step).wait_recv()
+    for step in (2, 1, 3):
+        slab_a.two(step).start()
+    slab_a.cross(0).start()
+    slab_b.wait_deep()
+    for step in range(1, 4):
+        slab_b.one(step).start()
 
     swap2.wait_recv()
     keep2.wait()
@@ -393,6 +392,11 @@
     for step in (1, 3, 2):
         slab_a.two(step).wait_recv()
         slab_a.cross(step).start()
+    for step in range(1, 4):
+        slab_b.one(step).wait_recv()
+    for step in (2, 1, 3):
+        slab_b.two(step).start()
+    slab_b.cross(0).start()
     for step in range(4):
         slab_a.cross(step).wait_recv()
 
@@ -431,6 +435,17 @@
         jnp.concatenate([jnp.where(seen[i] == within, named[i], 0.0) for i in range(2)], axis=1)
     ).astype(BF16)
 
+    @pl.when(wp_sends)
+    def _():
+        each(1, 16, lambda step: wpz(step, z // 4).wait_send())
+
+    for step in range(1, 4):
+        for copy in (wp1, wp2, wpc):
+            copy(step).wait_send()
+    wpc(0).wait_send()
+    slab_a.sent()
+    each(1, 16, lambda step: qkv_copy(step).wait_send())
+
     each(1, 16, lambda step: u_copy(step).wait_recv())
     u_own.wait()
     up_send[...] = (
@@ -472,45 +487,58 @@
     dn[...] = jnp.transpose(shared).astype(BF16)
     delta[...] = jnp.sum(shared * attn[...], axis=0, keepdims=True)
     dk_acc[...] = jnp.zeros_like(dk_acc)
-    dv_acc[...] = jnp.zeros_like(dv_acc)
 
     def place_lanes(ref, number):
         return ref.at[:, pl.ds(pl.multiple_of(number * 128, 128), 128)]
 
-    def b_copy(step):
-        to = lax.rem(chip + step, 16)
-        return remote(place_lanes(dq_t, to), dq_recv.at[chip], bs.at[step], br.at[step], on_chip(to))
-
-    def gradients(number):
-        block = lax.rem(chip // (QB // 128) + number, LENGTH // QB)
-        lanes = pl.ds(pl.multiple_of(block * QB, QB), QB)
-        weights = e_mat[:, lanes]
-        moved = dot(vn[...], d_out[:, lanes], NN) - delta[:, lanes]
-        slopes = (weights.astype(F32) * moved).astype(BF16)
-        dq_t[:, lanes] = (dot(kt[...], slopes, NN) * SCALE).astype(BF16)
+    def grad_copy(held, landed, send, recv):
+        def copy(step):
+            to = lax.rem(chip + step, 16)
+            return remote(place_lanes(held, to), landed.at[chip], send.at[step], recv.at[step], on_chip(to))
+
+        return copy
+
+    b_copy = grad_copy(dq_t, dq_recv, bs, br)
+    c_copy = grad_copy(dk_t, dk_recv, cs, cr)
+    v_copy = grad_copy(dv_t, dv_recv, vs, vr)
+
+    def block_of(number):
+        return lax.rem(chip // (QB // 128) + number, LENGTH // QB)
+
+    def send_block(block, copy):
         for part in range(QB // 128):
             step = lax.rem(QB // 128 * block + part - chip + 16, 16)
 
             @pl.when(step > 0)
             def _():
-                b_copy(step).start()
-
-        dv_acc[...] += dot(weights, dn[lanes, :], NN)
+                copy(step).start()
+
+    def value_gradients(number):
+        block = block_of(number)
+        held = pl.ds(pl.multiple_of(block * QB, QB), QB)
+        dv_t[:, held] = jnp.transpose(dot(e_mat[held, :], dn[...], NN)).astype(BF16)
+        send_block(block, v_copy)
+
+    each(0, LENGTH // QB, value_gradients)
+
+    def gradients(number):
+        block = block_of(number)
+        lanes = pl.ds(pl.multiple_of(block * QB, QB), QB)
+        moved = dot(vn[...], d_out[:, lanes], NN) - delta[:, lanes]
+        slopes = (e_mat[:, lanes].astype(F32) * moved).astype(BF16)
+        dq_t[:, lanes] = (dot(kt[...], slopes, NN) * SCALE).astype(BF16)
+        send_block(block, b_copy)
         dk_acc[...] += dot(slopes, qn[lanes, :], NN)
 
     each(0, LENGTH // QB, gradients)
-    turned = jnp.transpose(dk_acc[...] * SCALE)[0:40]
-    dkv_t[...] = jnp.concatenate([turned, jnp.transpose(dv_acc[...])[0:40]], axis=0).astype(BF16)
-
-    def c_copy(step):
-        to = lax.rem(chip + step, 16)
-        return remote(place_lanes(dkv_t, to), dkv_recv.at[chip], cs.at[step], cr.at[step], on_chip(to))
-
+    dk_t[...] = jnp.transpose(dk_acc[...] * SCALE).astype(BF16)
     each(1, 16, lambda step: c_copy(step).start())
-    b_own = pltpu.make_async_copy(place_lanes(dq_t, chip), dq_recv.at[chip], loc_sem.at[23])
-    c_own = pltpu.make_async_copy(place_lanes(dkv_t, chip), dkv_recv.at[chip], loc_sem.at[24])
-    b_own.start()
-    c_own.start()
+    own_copies = [
+        pltpu.make_async_copy(place_lanes(held, chip), landed.at[chip], loc_sem.at[23 + i])
+        for i, (held, landed) in enumerate(((dq_t, dq_recv), (dk_t, dk_recv), (dv_t, dv_recv)))
+    ]
+    for copy in own_copies:
+        copy.start()
 
     for step in (1, 3, 2):
         slab_b.two(step).wait_recv()
@@ -540,32 +568,23 @@
 
     each(0, 8, compact_b)
 
-    @pl.when(wp_sends)
-    def _():
-        each(1, 16, lambda step: wpz(step, z // 4).wait_send())
-
-    for step in range(1, 4):
-        for copy in (wp1, wp2, wpc):
-            copy(step).wait_send()
-    wpc(0).wait_send()
-    slab_a.sent()
     slab_b.sent()
 
     def sent(step):
-        for copy in (qkv_copy, u_copy, d_copy, b_copy):
+        for copy in (u_copy, d_copy, b_copy, v_copy):
             copy(step).wait_send()
 
     each(1, 16, sent)
     for copy in (swap1, swap2, swap3, edge_up, edge_down):
         copy.wait_send()
 
-    each(1, 16, lambda step: b_copy(step).wait_recv())
-    b_own.wait()
-    c_own.wait()
-    each(1, 16, lambda step: c_copy(step).wait_recv())
+    for copy in own_copies:
+        copy.wait()
+    for copy in (v_copy, b_copy, c_copy):
+        each(1, 16, lambda step: copy(step).wait_recv())
     d_normed = jnp.zeros((128, WIDTH), F32)
-    for i, (ref, low) in enumerate(((dq_recv, 0), (dkv_recv, 0), (dkv_recv, 40))):
-        turned = jnp.concatenate([ref[head].astype(F32)[low : low + 40] for head in range(16)], axis=0)
+    for i, ref in enumerate((dq_recv, dk_recv, dv_recv)):
+        turned = jnp.concatenate([ref[head].astype(F32)[0:40] for head in range(16)], axis=0)
         d_normed = d_normed + dot(jnp.transpose(turned).astype(BF16), w_full[1 + i], NT)
     scaled = d_normed * gain[...].reshape(1, WIDTH)
     d_layer = rstd * (
@@ -632,13 +651,13 @@
         ((LENGTH, 48), BF16), ((LENGTH, 48), BF16), ((LENGTH, 48), BF16),
         ((16, 16, WIDTH), BF16), ((16, 16, WIDTH), BF16), ((2, 64, WIDTH), BF16), ((2, 64, WIDTH), BF16),
         ((16, 48, 128), BF16), ((48, LENGTH), BF16), ((LENGTH, 48), BF16),
-        ((LENGTH, LENGTH), BF16), ((LENGTH, QB), F32), ((1, LENGTH), F32), ((1, LENGTH), F32), ((48, LENGTH), F32), ((LENGTH, 48), F32),
-        ((LENGTH, 48), F32), ((48, LENGTH), BF16), ((80, LENGTH), BF16), ((16, 48, 128), BF16),
-        ((16, 80, 128), BF16),
+        ((LENGTH, LENGTH), BF16), ((LENGTH, QB), F32), ((1, LENGTH), F32), ((1, LENGTH), F32),
+        ((48, LENGTH), F32), ((LENGTH, 48), F32), ((48, LENGTH), BF16), ((48, LENGTH), BF16),
+        ((48, LENGTH), BF16), ((16, 48, 128), BF16), ((16, 48, 128), BF16), ((16, 48, 128), BF16),
         ((5, 288, 128), F32), ((2, 16, WIDTH), BF16), ((128, WIDTH), BF16), ((2, 16, WIDTH), BF16),
         ((2, 128, 128), F32), ((128, 128), F32),
     ]
-    sems = [25, 16] + [4] * 7 + [16, 2] + [4] * 6 + [16, 2] + [4] * 6 + [4, 4] + [16] * 10 + [4, 4]
+    sems = [26, 16] + [4] * 7 + [16, 2] + [4] * 6 + [16, 2] + [4] * 6 + [4, 4] + [16] * 12 + [4, 4]
     result = pl.pallas_call(
         kernel,
         out_shape=jax.ShapeDtypeStruct((256, 128), F32),

time: 109 us -> 108 us (level)
  no operation moved by 1% of the time
where the time goes in v3:
time: 108 us
  Pallas kernels  106 us (98%)
  local copies, waits for them, and re-layouts  1.57 us (1%)
    pallas_call x1, Pallas kernels, per_device(): pl.pallas_call(kernel, out_shape=jax.ShapeDtypeStruct((256, 128), F32), i...  106 us

profile of v3, /device:TPU:1, one launch (start us, length us, event | category | flops | bytes accessed | tf_op | source)
XLA Modules:
  0.0 107.8 jit_solution(9637154837365432677)
XLA Ops:
  0.0 106.2 %shard_map.154 = f32[256,128]{1,0:T(8,128)} custom-call(s32[1,2]{1,0:T(1,128)} %counts.1, s32[2,64]{1,0:T(2,128)} %bitcast.11, bf16[192,2048]{1,0:T(8,128)(2,1)} %bitcast.9, bf16[1,64,2,640]{3,2,1,0:T(2,128)(2,1)} %q_in.1, bf16[1,64,2,640]{3,2,1,0:T(2,128)(2,1)} %k_in.1, bf16[1,64,2,640]{3,2,1,0:T(2,128)(2,1)} %v_in.1, bf16[1,64,2,640]{3,2,1,0:T(2,128)(2,1)} %c2_in.1, ...), custom_call_target="tpu_custom_call" | custom-call | tf_op jit(solution)/shard_map/pallas_call | solution.py:661
  106.2 1.6 %copy.18 = f32[1,128,2,128]{3,2,1,0:T(2,128)} copy(f32[1,128,2,128]{3,2,1,0:T(2,128)} %bitcast.10) | data formatting | bytes 262144

commit v4 on v3

--- a/solution.py
+++ b/solution.py
@@ -163,6 +163,100 @@
     keep1 = pltpu.make_async_copy(cl1.at[core], xb1.at[core], loc_sem.at[15])
     keep1.start()
 
+    for index in range(4):
+        @pl.when(kind + 4 * index != z)
+        def _():
+            wpz(1, index).wait_recv()
+
+    @pl.when(wp_sends)
+    def _():
+        wp_own.wait()
+
+    def wp1(step):
+        block = wp.at[wp_rows, pl.ds(pl.multiple_of(kind * 512, 128), 512)]
+        return remote(block, block, wp1_s.at[step], wp1_r.at[step], along_a(step))
+
+    for step in range(1, 4):
+        wp1(step).start()
+
+    group8 = a + 4 * core
+
+    class Slab:
+        def __init__(self, rows, held, full, sems, own_sem):
+            self.rows, self.held, self.full = rows, held, full
+            self.zs, self.zr, self.s1, self.r1, self.s2, self.r2, self.s3, self.r3 = sems
+            self.part = pl.ds(pl.multiple_of(b * rows, 16), rows)
+            self.sends = lax.rem(z, 8) == group8
+            self.own = pltpu.make_async_copy(
+                held.at[self.part, :], full.at[group8 * 2 + z // 8, self.part, :], own_sem
+            )
+
+        def deep(self, step, index):
+            return remote(
+                self.held.at[self.part, :], self.full.at[group8 * 2 + index, self.part, :],
+                self.zs.at[step], self.zr.at[index], along_z(step),
+            )
+
+        def start_deep(self):
+            @pl.when(self.sends)
+            def _():
+                each(1, 16, lambda step: self.deep(step, z // 8).start())
+                self.own.start()
+
+        def wait_deep(self):
+            for index in range(2):
+                @pl.when(group8 + 8 * index != z)
+                def _():
+                    self.deep(1, index).wait_recv()
+
+            @pl.when(self.sends)
+            def _():
+                self.own.wait()
+
+        def one(self, step):
+            block = self.full.at[pl.ds(group8 * 2, 2), self.part, :]
+            return remote(block, block, self.s1.at[step], self.r1.at[step], along_a(step))
+
+        def band(self, number):
+            return self.full.at[
+                pl.ds(core * 8, 8), pl.ds(pl.multiple_of(number * self.rows, 16), self.rows), :
+            ]
+
+        def two(self, step):
+            return remote(self.band(b), self.band(b), self.s2.at[step], self.r2.at[step], along_b(step))
+
+        def cross(self, step):
+            band = self.band(lax.rem(b - step + 4, 4))
+            return remote(band, band, self.s3.at[step], self.r3.at[step], sibling)
+
+        def sent(self):
+            @pl.when(self.sends)
+            def _():
+                each(1, 16, lambda step: self.deep(step, z // 8).wait_send())
+
+            for step in range(1, 4):
+                self.one(step).wait_send()
+                self.two(step).wait_send()
+            for step in range(4):
+                self.cross(step).wait_send()
+
+    slab_a = Slab(
+        16, a_slab, wa, (waz_s, waz_r, wa1_s, wa1_r, wa2_s, wa2_r, wac_s, wac_r), loc_sem.at[16]
+    )
+    slab_b = Slab(
+        64, b_slab, wb, (wbz_s, wbz_r, wb1_s, wb1_r, wb2_s, wb2_r, wbc_s, wbc_r), loc_sem.at[17]
+    )
+    loaded(3)
+    loaded(4)
+    parts = [wo_loc[...].astype(F32)] + [wc1_loc[i].astype(F32) for i in range(3)]
+    a_slab[...] = jnp.concatenate(parts, axis=0).astype(BF16)
+    slab_a.start_deep()
+    loaded(5)
+    loaded(6)
+    parts = [wqkv_loc[i].astype(F32) for i in range(3)] + [wc2_loc[i].astype(F32) for i in range(3)]
+    b_slab[...] = jnp.concatenate(parts + [jnp.zeros((16, WIDTH), F32)], axis=0).astype(BF16)
+    slab_b.start_deep()
+
     swap1.wait_recv()
     keep1.wait()
     zero_rows = jnp.zeros((8, 128), F32)
@@ -185,100 +279,6 @@
     each(1, 16, lambda step: qkv_copy(step).start())
     qkv_own = pltpu.make_async_copy(head_send.at[chip], qkv.at[:, chip_lanes], loc_sem.at[18])
     qkv_own.start()
-
-    for index in range(4):
-        @pl.when(kind + 4 * index != z)
-        def _():
-            wpz(1, index).wait_recv()
-
-    @pl.when(wp_sends)
-    def _():
-        wp_own.wait()
-
-    def wp1(step):
-        block = wp.at[wp_rows, pl.ds(pl.multiple_of(kind * 512, 128), 512)]
-        return remote(block, block, wp1_s.at[step], wp1_r.at[step], along_a(step))
-
-    for step in range(1, 4):
-        wp1(step).start()
-
-    group8 = a + 4 * core
-
-    class Slab:
-        def __init__(self, rows, held, full, sems, own_sem):
-            self.rows, self.held, self.full = rows, held, full
-            self.zs, self.zr, self.s1, self.r1, self.s2, self.r2, self.s3, self.r3 = sems
-            self.part = pl.ds(pl.multiple_of(b * rows, 16), rows)
-            self.sends = lax.rem(z, 8) == group8
-            self.own = pltpu.make_async_copy(
-                held.at[self.part, :], full.at[group8 * 2 + z // 8, self.part, :], own_sem
-            )
-
-        def deep(self, step, index):
-            return remote(
-                self.held.at[self.part, :], self.full.at[group8 * 2 + index, self.part, :],
-                self.zs.at[step], self.zr.at[index], along_z(step),
-            )
-
-        def start_deep(self):
-            @pl.when(self.sends)
-            def _():
-                each(1, 16, lambda step: self.deep(step, z // 8).start())
-                self.own.start()
-
-        def wait_deep(self):
-            for index in range(2):
-                @pl.when(group8 + 8 * index != z)
-                def _():
-                    self.deep(1, index).wait_recv()
-
-            @pl.when(self.sends)
-            def _():
-                self.own.wait()
-
-        def one(self, step):
-            block = self.full.at[pl.ds(group8 * 2, 2), self.part, :]
-            return remote(block, block, self.s1.at[step], self.r1.at[step], along_a(step))
-
-        def band(self, number):
-            return self.full.at[
-                pl.ds(core * 8, 8), pl.ds(pl.multiple_of(number * self.rows, 16), self.rows), :
-            ]
-
-        def two(self, step):
-            return remote(self.band(b), self.band(b), self.s2.at[step], self.r2.at[step], along_b(step))
-
-        def cross(self, step):
-            band = self.band(lax.rem(b - step + 4, 4))
-            return remote(band, band, self.s3.at[step], self.r3.at[step], sibling)
-
-        def sent(self):
-            @pl.when(self.sends)
-            def _():
-                each(1, 16, lambda step: self.deep(step, z // 8).wait_send())
-
-            for step in range(1, 4):
-                self.one(step).wait_send()
-                self.two(step).wait_send()
-            for step in range(4):
-                self.cross(step).wait_send()
-
-    slab_a = Slab(
-        16, a_slab, wa, (waz_s, waz_r, wa1_s, wa1_r, wa2_s, wa2_r, wac_s, wac_r), loc_sem.at[16]
-    )
-    slab_b = Slab(
-        64, b_slab, wb, (wbz_s, wbz_r, wb1_s, wb1_r, wb2_s, wb2_r, wbc_s, wbc_r), loc_sem.at[17]
-    )
-    loaded(3)
-    loaded(4)
-    parts = [wo_loc[...].astype(F32)] + [wc1_loc[i].astype(F32) for i in range(3)]
-    a_slab[...] = jnp.concatenate(parts, axis=0).astype(BF16)
-    slab_a.start_deep()
-    loaded(5)
-    loaded(6)
-    parts = [wqkv_loc[i].astype(F32) for i in range(3)] + [wc2_loc[i].astype(F32) for i in range(3)]
-    b_slab[...] = jnp.concatenate(parts + [jnp.zeros((16, WIDTH), F32)], axis=0).astype(BF16)
-    slab_b.start_deep()
 
     for step in range(1, 4):
         wp1(step).wait_recv()

time: 108 us -> 112 us (1.037)
  Pallas kernels: 106 us -> 110 us
    pallas_call x1, Pallas kernels: 106 us -> 110 us  [per_device(): pl.pallas_call(kernel, out_shape=jax.ShapeDtypeStruct((256, 128), F32), i...]
where the time goes in v4:
time: 112 us
  Pallas kernels  110 us (98%)
  local copies, waits for them, and re-layouts  1.57 us (1%)
    pallas_call x1, Pallas kernels, per_device(): pl.pallas_call(kernel, out_shape=jax.ShapeDtypeStruct((256, 128), F32), i...  110 us

profile of v4, /device:TPU:1, one launch (start us, length us, event | category | flops | bytes accessed | tf_op | source)
XLA Modules:
  0.0 111.7 jit_solution(612660223721188671)
XLA Ops:
  0.0 110.2 %shard_map.154 = f32[256,128]{1,0:T(8,128)} custom-call(s32[1,2]{1,0:T(1,128)} %counts.1, s32[2,64]{1,0:T(2,128)} %bitcast.11, bf16[192,2048]{1,0:T(8,128)(2,1)} %bitcast.9, bf16[1,64,2,640]{3,2,1,0:T(2,128)(2,1)} %q_in.1, bf16[1,64,2,640]{3,2,1,0:T(2,128)(2,1)} %k_in.1, bf16[1,64,2,640]{3,2,1,0:T(2,128)(2,1)} %v_in.1, bf16[1,64,2,640]{3,2,1,0:T(2,128)(2,1)} %c2_in.1, ...), custom_call_target="tpu_custom_call" | custom-call | tf_op jit(solution)/shard_map/pallas_call | solution.py:661
  110.2 1.6 %copy.18 = f32[1,128,2,128]{3,2,1,0:T(2,128)} copy(f32[1,128,2,128]{3,2,1,0:T(2,128)} %bitcast.10) | data formatting | bytes 262144
